TPU v7x, 32 devices: a whole 2x2x4 slice. The times are simulated.
32 devices in a mesh: groups: 2 (over x), leaf: 16 (over z, y, core).
Axes of the slice: x: 2, y: 2, z: 4, core: 2. Of those that a mesh axis runs over, the one named last changes fastest.
Arguments:
- points: bfloat16 [8, 131072], P(None, ('groups', 'leaf')), parts along dimension 1, may hold values from -3.5 to 3.5
- weights: bfloat16 [64, 131072], P(None, ('groups', 'leaf')), parts along dimension 1, may hold values from -6 to 6
- interpolation: bfloat16 [256, 512, 256], P(('groups', 'leaf')), parts along dimension 0, may hold values from -0.25 to 0.25
- skeleton: int32 [256, 256], P(('groups', 'leaf')), parts along dimension 0, may hold values from 0 to 511, as said below
- near_lists: int32 [256, 8], P(('groups', 'leaf')), parts along dimension 0, may hold values from 0 to 127, as said below
- far_lists: int32 [256, 12], P(('groups', 'leaf')), parts along dimension 0, may hold values from 0 to 127, as said below
Outputs:
- kernel_product: float32 [64, 131072], P(None, ('groups', 'leaf')), parts along dimension 1
- derivative_product: float32 [64, 131072], P(None, ('groups', 'leaf')), parts along dimension 1
There are 2 independent parts, one for each index of `groups`. A program takes and returns all parts, laid end to end along the dimension named above; each array names one. Nothing has to cross between parts.
Inputs may be any that keep to these rules, and one draw needn't show every extreme that they name: `skeleton`: each row holds 256 distinct positions. near_lists[j] begins with j and holds 8 distinct leaves, all within 8 leaves of j. Leaf j lies on device j // 8. far_lists[j] holds 12 distinct leaves, none on the device of leaf j or on the devices next to it; the far lists of one device's 8 leaves name at most 8 leaves of any one device, and exactly 8 of some device.
All inputs are finite; a program needn't handle non-finite values.
Results may differ from a plain program's by a relative error of at most 0.0036.
Values may be sent and summed in bfloat16 or wider, within the bound.
A program may use at most 128 MiB of HBM per device.

v0:
```python
import jax
import jax.numpy as jnp
from jax import lax
from jax.sharding import PartitionSpec as P

amplitude = 0.03
length_sq = 4.0


def extended_2(cells, sides, width):
    for axis, dim in sides:
        count = lax.axis_size(axis)
        ends = count - 1
        head = lax.slice_in_dim(cells, 0, width, axis=dim)
        tail = lax.slice_in_dim(cells, cells.shape[dim] - width, cells.shape[dim], axis=dim)
        cells = jnp.concatenate(
            [
                lax.ppermute(tail, axis, [(i, (i + 1) % count) for i in range(ends)]),
                cells,
                lax.ppermute(head, axis, [((i + 1) % count, i) for i in range(ends)]),
            ],
            axis=dim,
        )
    return cells


def kernel_tiles(source, target):
    source_wide = source.astype(jnp.float32)
    target_wide = target.astype(jnp.float32)
    distance = jnp.zeros((source.shape[1], target.shape[1]), jnp.float32)
    for coordinate in range(source.shape[0]):
        offset = source_wide[coordinate][:, None] - target_wide[coordinate][None, :]
        distance = distance + offset * offset
    kernel = amplitude * jnp.exp(distance * (-0.5 / length_sq))
    slope = kernel * distance / length_sq
    return jnp.concatenate([kernel.astype(jnp.bfloat16), slope.astype(jnp.bfloat16)], axis=1)


def leaf_product(target, near_blocks, far_payload, coord_count):
    near_flat = near_blocks.reshape(near_blocks.shape[0], -1)
    tiles = kernel_tiles(near_flat[:coord_count], target)
    near_part = jnp.dot(near_flat[coord_count:], tiles, preferred_element_type=jnp.float32)
    far_flat = far_payload.transpose(1, 0, 2).reshape(far_payload.shape[1], -1)
    far_tiles = kernel_tiles(far_flat[:coord_count], target)
    far_part = jnp.dot(far_flat[coord_count:], far_tiles, preferred_element_type=jnp.float32)
    return near_part + far_part


def skeleton_payload(points, weights, interpolation, skeleton):
    leaves = interpolation.shape[0]
    leaf_size = interpolation.shape[1]
    coord_count = points.shape[0]
    coords = points.reshape(coord_count, leaves, leaf_size).transpose(1, 0, 2)
    positions = jnp.arange(leaf_size, dtype=jnp.int32)
    selector = (skeleton[:, :, None] == positions[None, None, :]).astype(jnp.bfloat16)
    chosen = jnp.einsum(
        "bcl,brl->bcr", coords, selector, preferred_element_type=jnp.float32
    ).astype(jnp.bfloat16)
    per_leaf = weights.reshape(weights.shape[0], leaves, leaf_size).transpose(1, 0, 2)
    projected = jnp.einsum(
        "bhl,blr->bhr", per_leaf, interpolation, preferred_element_type=jnp.float32
    )
    return jnp.concatenate([chosen, projected.astype(jnp.bfloat16)], axis=1)


def local(points, weights, interpolation, skeleton, near_lists, far_lists):
    position = lax.axis_index("leaf")
    leaf_dev = interpolation.shape[0]
    leaf_size = interpolation.shape[1]
    coord_count = points.shape[0]
    rhs_count = weights.shape[0]
    far_count = far_lists.shape[1]
    near_count = near_lists.shape[1]
    requests = leaf_dev * far_count
    payload = skeleton_payload(points, weights, interpolation, skeleton)
    wanted = far_lists.reshape(requests)
    everything = lax.all_gather(payload, "leaf", axis=0, tiled=True)
    fetched = jnp.take(everything, wanted, axis=0)
    stacked = jnp.concatenate([points, weights], axis=0)
    extended = extended_2(stacked, (("leaf", 1),), leaf_dev * leaf_size)
    local_near = near_lists - (position - 1) * leaf_dev
    targets = points.reshape(coord_count, leaf_dev, leaf_size).transpose(1, 0, 2)
    far_blocks = fetched.reshape((leaf_dev, far_count) + payload.shape[1:])

    def one_leaf(inputs):
        target, near_ids, far_payload = inputs
        pieces = [
            lax.dynamic_slice_in_dim(extended, near_ids[slot] * leaf_size, leaf_size, 1)
            for slot in range(near_count)
        ]
        near_blocks = jnp.stack(pieces, axis=1)
        return leaf_product(target, near_blocks, far_payload, coord_count)

    results = lax.map(one_leaf, (targets, local_near, far_blocks))
    kernel_product = results[:, :, :leaf_size].transpose(1, 0, 2).reshape(rhs_count, -1)
    derivative_product = results[:, :, leaf_size:].transpose(1, 0, 2).reshape(rhs_count, -1)
    return (kernel_product, derivative_product)


def solution(mesh):
    placed = (
        P(None, ("groups", "leaf")),
        P(None, ("groups", "leaf")),
        P(("groups", "leaf"), None, None),
        P(("groups", "leaf"), None),
        P(("groups", "leaf"), None),
        P(("groups", "leaf"), None),
    )
    return jax.shard_map(
        local,
        mesh=mesh,
        in_specs=placed,
        out_specs=(P(None, ("groups", "leaf")), P(None, ("groups", "leaf"))),
        check_vma=False,
    )
```

profile of v0, /device:TPU:16, one launch (start us, length us, event | category | flops | bytes accessed | tf_op | source)
XLA Modules:
  0.0 365.8 jit_solution(12262813932567465794)
XLA Ops:
  7.3 1.5 copy-done
  8.8 1.5 convolution_convert_fusion
  10.3 1.7 fusion.24
  12.9 2.8 collective-permute-start.1
  15.7 1.9 collective-permute-start
  17.7 5.3 %collective-permute-done.1 = bf16[72,4096]{1,0:T(8,128)(2,1)} collective-permute-done((bf16[72,4096]{1,0:T(8,128)(2,1)S(1)}, bf16[72,4096]{1,0:T(8,128)(2,1)}, u32[]{:S(2)}, u32[]{:S(2)}) %collective-permute-start.1) | collective-permute-done | bytes 589856 | tf_op jit(solution)/shard_map/ppermute | solution.py:20
  23.1 13.4 %collective-permute-done = bf16[72,4096]{1,0:T(8,128)(2,1)} collective-permute-done((bf16[72,4096]{1,0:T(8,128)(2,1)S(1)}, bf16[72,4096]{1,0:T(8,128)(2,1)}, u32[]{:S(2)}, u32[]{:S(2)}) %collective-permute-start) | collective-permute-done | bytes 589856 | tf_op jit(solution)/shard_map/ppermute | solution.py:18
  36.5 2.5 pad_maximum_fusion
  39.0 31.0 %all-gather.2.cloned.1.call-done = bf16[128,72,256]{2,1,0:T(8,128)(2,1)} async-done(((bf16[8,72,256]{2,1,0:T(8,128)(2,1)}), bf16[128,72,256]{2,1,0:T(8,128)(2,1)}) %all-gather.2.cloned.1.call-update) | async-done | bytes 4718608 | tf_op jit(solution)/shard_map/all_gather | solution.py:77
  70.1 5.1 %gather_fusion = bf16[96,72,256]{2,1,0:T(8,128)(2,1)} fusion(bf16[128,72,256]{2,1,0:T(8,128)(2,1)} %all-gather.2.cloned.1.call-done, s32[1024]{0:T(1024)S(1)} %pad_clamp_fusion), kind=kCustom, calls=%fused_computation | custom fusion | bytes 7078272 | tf_op jit(solution)/shard_map/jit(_take)/gather | solution.py:78
  75.1 5.0 %copy_select_fusion = bf16[8,12,72,256]{3,1,2,0:T(8,128)(2,1)} fusion(bf16[8,12,72,256]{3,2,1,0:T(8,128)(2,1)} %bitcast.161, pred[8,12]{1,0:T(8,128)(4,1)S(1)} %compare_and_fusion), kind=kLoop, calls=%fused_computation.36 | loop fusion | flops 1769472 | bytes 7077984 | tf_op jit(solution)/shard_map/jit(_take)/select_n | solution.py:78
  80.1 274.9 %while.10 = (s32[]{:T(128)}, f32[8,64,1024]{2,1,0:T(8,128)}, s32[8,8]{1,0:T(8,128)S(1)}, bf16[72,12288]{1,0:T(8,128)(2,1)}, bf16[8,8,512]{2,1,0:T(8,128)(2,1)S(1...) while((s32[]{:T(128)}, f32[8,64,1024]{2,1,0:T(8,128)}, ...), condition=%wide.region_1.2_spmd, body=%wide.region_0.1_spmd.sunk | while | flops 1075441664 | bytes 38118028 | solution.py:94
  93.2 9.3 %fusion.54 = (bf16[4096,512]{1,0:T(8,128)(2,1)S(1)}, bf16[4096,512]{1,0:T(8,128)(2,1)S(1)}) fusion(f32[512]{0:T(512)S(1)} %bitcast.177, f32[4096]{0:T(1024)S(1)} %bitcast.166, f32[512]{0:T(512)S(1)} %bitcast.179, f32[4096]{0:T(1024)S(1)} %bitcast.167, f32[512]{0:T(512)S(1)} %bitcast.181, f32[4096]{0:T(1024)S(1)} %bitcast.168, f32[512]{0:T(512)S(1)} %bitcast.183, ...), kind=kLoop, calls=%fused_computation.7.clone.1 | loop fusion | flops 60817408 | bytes 8536064 | tf_op jit(solution)/shard_map/while/body/eval_jaxpr/convert_element_type | solution.py:36
  102.5 1.5 fusion.55
  105.5 7.1 %fusion.57 = (bf16[3072,512]{1,0:T(8,128)(2,1)S(1)}, bf16[3072,512]{1,0:T(8,128)(2,1)S(1)}) fusion(f32[512]{0:T(512)S(1)} %bitcast.178, f32[3072]{0:T(1024)S(1)} %sub.614, f32[512]{0:T(512)S(1)} %bitcast.180, f32[3072]{0:T(1024)S(1)} %sub.615, f32[512]{0:T(512)S(1)} %bitcast.182, f32[3072]{0:T(1024)S(1)} %sub.616, f32[512]{0:T(512)S(1)} %bitcast.184, ...), kind=kLoop, calls=%fused_computation.15.clone.1 | loop fusion | flops 45613056 | bytes 6406144 | tf_op jit(solution)/shard_map/while/body/eval_jaxpr/convert_element_type | solution.py:36
  112.6 1.9 fusion.58
  127.6 9.3 %fusion.54 = (bf16[4096,512]{1,0:T(8,128)(2,1)S(1)}, bf16[4096,512]{1,0:T(8,128)(2,1)S(1)}) fusion(f32[512]{0:T(512)S(1)} %bitcast.177, f32[4096]{0:T(1024)S(1)} %bitcast.166, f32[512]{0:T(512)S(1)} %bitcast.179, f32[4096]{0:T(1024)S(1)} %bitcast.167, f32[512]{0:T(512)S(1)} %bitcast.181, f32[4096]{0:T(1024)S(1)} %bitcast.168, f32[512]{0:T(512)S(1)} %bitcast.183, ...), kind=kLoop, calls=%fused_computation.7.clone.1 | loop fusion | flops 60817408 | bytes 8536064 | tf_op jit(solution)/shard_map/while/body/eval_jaxpr/convert_element_type | solution.py:36
  136.9 1.5 fusion.55
  139.9 7.1 %fusion.57 = (bf16[3072,512]{1,0:T(8,128)(2,1)S(1)}, bf16[3072,512]{1,0:T(8,128)(2,1)S(1)}) fusion(f32[512]{0:T(512)S(1)} %bitcast.178, f32[3072]{0:T(1024)S(1)} %sub.614, f32[512]{0:T(512)S(1)} %bitcast.180, f32[3072]{0:T(1024)S(1)} %sub.615, f32[512]{0:T(512)S(1)} %bitcast.182, f32[3072]{0:T(1024)S(1)} %sub.616, f32[512]{0:T(512)S(1)} %bitcast.184, ...), kind=kLoop, calls=%fused_computation.15.clone.1 | loop fusion | flops 45613056 | bytes 6406144 | tf_op jit(solution)/shard_map/while/body/eval_jaxpr/convert_element_type | solution.py:36
  147.0 1.9 fusion.58
  162.0 9.3 %fusion.54 = (bf16[4096,512]{1,0:T(8,128)(2,1)S(1)}, bf16[4096,512]{1,0:T(8,128)(2,1)S(1)}) fusion(f32[512]{0:T(512)S(1)} %bitcast.177, f32[4096]{0:T(1024)S(1)} %bitcast.166, f32[512]{0:T(512)S(1)} %bitcast.179, f32[4096]{0:T(1024)S(1)} %bitcast.167, f32[512]{0:T(512)S(1)} %bitcast.181, f32[4096]{0:T(1024)S(1)} %bitcast.168, f32[512]{0:T(512)S(1)} %bitcast.183, ...), kind=kLoop, calls=%fused_computation.7.clone.1 | loop fusion | flops 60817408 | bytes 8536064 | tf_op jit(solution)/shard_map/while/body/eval_jaxpr/convert_element_type | solution.py:36
  171.3 1.5 fusion.55
  172.8 1.1 dynamic-slice_bitcast_fusion.2
  174.3 7.1 %fusion.57 = (bf16[3072,512]{1,0:T(8,128)(2,1)S(1)}, bf16[3072,512]{1,0:T(8,128)(2,1)S(1)}) fusion(f32[512]{0:T(512)S(1)} %bitcast.178, f32[3072]{0:T(1024)S(1)} %sub.614, f32[512]{0:T(512)S(1)} %bitcast.180, f32[3072]{0:T(1024)S(1)} %sub.615, f32[512]{0:T(512)S(1)} %bitcast.182, f32[3072]{0:T(1024)S(1)} %sub.616, f32[512]{0:T(512)S(1)} %bitcast.184, ...), kind=kLoop, calls=%fused_computation.15.clone.1 | loop fusion | flops 45613056 | bytes 6406144 | tf_op jit(solution)/shard_map/while/body/eval_jaxpr/convert_element_type | solution.py:36
  181.4 1.9 fusion.58
  196.3 9.3 %fusion.54 = (bf16[4096,512]{1,0:T(8,128)(2,1)S(1)}, bf16[4096,512]{1,0:T(8,128)(2,1)S(1)}) fusion(f32[512]{0:T(512)S(1)} %bitcast.177, f32[4096]{0:T(1024)S(1)} %bitcast.166, f32[512]{0:T(512)S(1)} %bitcast.179, f32[4096]{0:T(1024)S(1)} %bitcast.167, f32[512]{0:T(512)S(1)} %bitcast.181, f32[4096]{0:T(1024)S(1)} %bitcast.168, f32[512]{0:T(512)S(1)} %bitcast.183, ...), kind=kLoop, calls=%fused_computation.7.clone.1 | loop fusion | flops 60817408 | bytes 8536064 | tf_op jit(solution)/shard_map/while/body/eval_jaxpr/convert_element_type | solution.py:36
  205.7 1.5 fusion.55
  207.2 1.1 dynamic-slice_bitcast_fusion.2
  208.6 7.1 %fusion.57 = (bf16[3072,512]{1,0:T(8,128)(2,1)S(1)}, bf16[3072,512]{1,0:T(8,128)(2,1)S(1)}) fusion(f32[512]{0:T(512)S(1)} %bitcast.178, f32[3072]{0:T(1024)S(1)} %sub.614, f32[512]{0:T(512)S(1)} %bitcast.180, f32[3072]{0:T(1024)S(1)} %sub.615, f32[512]{0:T(512)S(1)} %bitcast.182, f32[3072]{0:T(1024)S(1)} %sub.616, f32[512]{0:T(512)S(1)} %bitcast.184, ...), kind=kLoop, calls=%fused_computation.15.clone.1 | loop fusion | flops 45613056 | bytes 6406144 | tf_op jit(solution)/shard_map/while/body/eval_jaxpr/convert_element_type | solution.py:36
  215.7 1.9 fusion.58
  230.7 9.3 %fusion.54 = (bf16[4096,512]{1,0:T(8,128)(2,1)S(1)}, bf16[4096,512]{1,0:T(8,128)(2,1)S(1)}) fusion(f32[512]{0:T(512)S(1)} %bitcast.177, f32[4096]{0:T(1024)S(1)} %bitcast.166, f32[512]{0:T(512)S(1)} %bitcast.179, f32[4096]{0:T(1024)S(1)} %bitcast.167, f32[512]{0:T(512)S(1)} %bitcast.181, f32[4096]{0:T(1024)S(1)} %bitcast.168, f32[512]{0:T(512)S(1)} %bitcast.183, ...), kind=kLoop, calls=%fused_computation.7.clone.1 | loop fusion | flops 60817408 | bytes 8536064 | tf_op jit(solution)/shard_map/while/body/eval_jaxpr/convert_element_type | solution.py:36
  240.0 1.5 fusion.55
  243.0 7.1 %fusion.57 = (bf16[3072,512]{1,0:T(8,128)(2,1)S(1)}, bf16[3072,512]{1,0:T(8,128)(2,1)S(1)}) fusion(f32[512]{0:T(512)S(1)} %bitcast.178, f32[3072]{0:T(1024)S(1)} %sub.614, f32[512]{0:T(512)S(1)} %bitcast.180, f32[3072]{0:T(1024)S(1)} %sub.615, f32[512]{0:T(512)S(1)} %bitcast.182, f32[3072]{0:T(1024)S(1)} %sub.616, f32[512]{0:T(512)S(1)} %bitcast.184, ...), kind=kLoop, calls=%fused_computation.15.clone.1 | loop fusion | flops 45613056 | bytes 6406144 | tf_op jit(solution)/shard_map/while/body/eval_jaxpr/convert_element_type | solution.py:36
  250.1 1.9 fusion.58
  265.1 9.3 %fusion.54 = (bf16[4096,512]{1,0:T(8,128)(2,1)S(1)}, bf16[4096,512]{1,0:T(8,128)(2,1)S(1)}) fusion(f32[512]{0:T(512)S(1)} %bitcast.177, f32[4096]{0:T(1024)S(1)} %bitcast.166, f32[512]{0:T(512)S(1)} %bitcast.179, f32[4096]{0:T(1024)S(1)} %bitcast.167, f32[512]{0:T(512)S(1)} %bitcast.181, f32[4096]{0:T(1024)S(1)} %bitcast.168, f32[512]{0:T(512)S(1)} %bitcast.183, ...), kind=kLoop, calls=%fused_computation.7.clone.1 | loop fusion | flops 60817408 | bytes 8536064 | tf_op jit(solution)/shard_map/while/body/eval_jaxpr/convert_element_type | solution.py:36
  274.4 1.5 fusion.55
  275.9 1.1 dynamic-slice_bitcast_fusion.2
  277.4 7.1 %fusion.57 = (bf16[3072,512]{1,0:T(8,128)(2,1)S(1)}, bf16[3072,512]{1,0:T(8,128)(2,1)S(1)}) fusion(f32[512]{0:T(512)S(1)} %bitcast.178, f32[3072]{0:T(1024)S(1)} %sub.614, f32[512]{0:T(512)S(1)} %bitcast.180, f32[3072]{0:T(1024)S(1)} %sub.615, f32[512]{0:T(512)S(1)} %bitcast.182, f32[3072]{0:T(1024)S(1)} %sub.616, f32[512]{0:T(512)S(1)} %bitcast.184, ...), kind=kLoop, calls=%fused_computation.15.clone.1 | loop fusion | flops 45613056 | bytes 6406144 | tf_op jit(solution)/shard_map/while/body/eval_jaxpr/convert_element_type | solution.py:36
  284.5 1.9 fusion.58
  299.4 9.3 %fusion.54 = (bf16[4096,512]{1,0:T(8,128)(2,1)S(1)}, bf16[4096,512]{1,0:T(8,128)(2,1)S(1)}) fusion(f32[512]{0:T(512)S(1)} %bitcast.177, f32[4096]{0:T(1024)S(1)} %bitcast.166, f32[512]{0:T(512)S(1)} %bitcast.179, f32[4096]{0:T(1024)S(1)} %bitcast.167, f32[512]{0:T(512)S(1)} %bitcast.181, f32[4096]{0:T(1024)S(1)} %bitcast.168, f32[512]{0:T(512)S(1)} %bitcast.183, ...), kind=kLoop, calls=%fused_computation.7.clone.1 | loop fusion | flops 60817408 | bytes 8536064 | tf_op jit(solution)/shard_map/while/body/eval_jaxpr/convert_element_type | solution.py:36
  308.8 1.5 fusion.55
  311.7 7.1 %fusion.57 = (bf16[3072,512]{1,0:T(8,128)(2,1)S(1)}, bf16[3072,512]{1,0:T(8,128)(2,1)S(1)}) fusion(f32[512]{0:T(512)S(1)} %bitcast.178, f32[3072]{0:T(1024)S(1)} %sub.614, f32[512]{0:T(512)S(1)} %bitcast.180, f32[3072]{0:T(1024)S(1)} %sub.615, f32[512]{0:T(512)S(1)} %bitcast.182, f32[3072]{0:T(1024)S(1)} %sub.616, f32[512]{0:T(512)S(1)} %bitcast.184, ...), kind=kLoop, calls=%fused_computation.15.clone.1 | loop fusion | flops 45613056 | bytes 6406144 | tf_op jit(solution)/shard_map/while/body/eval_jaxpr/convert_element_type | solution.py:36
  318.8 1.9 fusion.58
  333.8 9.3 %fusion.54 = (bf16[4096,512]{1,0:T(8,128)(2,1)S(1)}, bf16[4096,512]{1,0:T(8,128)(2,1)S(1)}) fusion(f32[512]{0:T(512)S(1)} %bitcast.177, f32[4096]{0:T(1024)S(1)} %bitcast.166, f32[512]{0:T(512)S(1)} %bitcast.179, f32[4096]{0:T(1024)S(1)} %bitcast.167, f32[512]{0:T(512)S(1)} %bitcast.181, f32[4096]{0:T(1024)S(1)} %bitcast.168, f32[512]{0:T(512)S(1)} %bitcast.183, ...), kind=kLoop, calls=%fused_computation.7.clone.1 | loop fusion | flops 60817408 | bytes 8536064 | tf_op jit(solution)/shard_map/while/body/eval_jaxpr/convert_element_type | solution.py:36
  343.1 1.5 fusion.55
  346.1 7.1 %fusion.57 = (bf16[3072,512]{1,0:T(8,128)(2,1)S(1)}, bf16[3072,512]{1,0:T(8,128)(2,1)S(1)}) fusion(f32[512]{0:T(512)S(1)} %bitcast.178, f32[3072]{0:T(1024)S(1)} %sub.614, f32[512]{0:T(512)S(1)} %bitcast.180, f32[3072]{0:T(1024)S(1)} %sub.615, f32[512]{0:T(512)S(1)} %bitcast.182, f32[3072]{0:T(1024)S(1)} %sub.616, f32[512]{0:T(512)S(1)} %bitcast.184, ...), kind=kLoop, calls=%fused_computation.15.clone.1 | loop fusion | flops 45613056 | bytes 6406144 | tf_op jit(solution)/shard_map/while/body/eval_jaxpr/convert_element_type | solution.py:36
  353.2 1.9 fusion.58
  355.1 1.8 slice_bitcast_fusion.1
  (251 shorter events, 74.8 us)
Async XLA Ops:
  7.2 1.6 copy-start
  7.2 5.7 %copy-start.1 = (bf16[64,4096]{1,0:T(8,128)(2,1)S(1)}, bf16[64,4096]{1,0:T(8,128)(2,1)}, u32[]{:S(2)}) copy-start(bf16[64,4096]{1,0:T(8,128)(2,1)} %param.9) | copy-start | bytes 1572868
  7.2 5.6 %copy-start.2 = (bf16[8,4096]{1,0:T(8,128)(2,1)S(1)}, bf16[8,4096]{1,0:T(8,128)(2,1)}, u32[]{:S(2)}) copy-start(bf16[8,4096]{1,0:T(8,128)(2,1)} %param.8) | copy-start | bytes 196612
  7.2 10.4 %copy-start.3 = (s32[8,12]{1,0:T(8,128)S(1)}, s32[8,12]{1,0:T(8,128)}, u32[]{:S(2)}) copy-start(s32[8,12]{1,0:T(8,128)} %param.13) | copy-start | bytes 1156
  7.2 10.5 %copy-start.4 = (s32[8,8]{1,0:T(8,128)S(1)}, s32[8,8]{1,0:T(8,128)}, u32[]{:S(2)}) copy-start(s32[8,8]{1,0:T(8,128)} %param.12) | copy-start | bytes 772
  7.2 62.8 %all-gather.2.cloned.1.call-start = ((), (), s32[]{:S(2)}) async-start(), calls=%async_computation | async-start | bytes 5013504 | tf_op jit(solution)/shard_map/all_gather | solution.py:77
  12.9 10.2 %collective-permute-start.1 = (bf16[72,4096]{1,0:T(8,128)(2,1)S(1)}, bf16[72,4096]{1,0:T(8,128)(2,1)}, u32[]{:S(2)}, u32[]{:S(2)}) collective-permute-start(bf16[72,4096]{1,0:T(8,128)(2,1)S(1)} %constant_dynamic-update-slice_fusion), channel_id=1, source_target_pairs={{1,0},{2,1},{3,2},{4,3},{5,4},{6,5},{7,6},{8,7},{9,8},{10,9},{11,1... | collective-permute-start | bytes 1769480 | tf_op jit(solution)/shard_map/ppermute | solution.py:20
  15.7 20.8 %collective-permute-start = (bf16[72,4096]{1,0:T(8,128)(2,1)S(1)}, bf16[72,4096]{1,0:T(8,128)(2,1)}, u32[]{:S(2)}, u32[]{:S(2)}) collective-permute-start(bf16[72,4096]{1,0:T(8,128)(2,1)S(1)} %constant_dynamic-update-slice_fusion), channel_id=1, source_target_pairs={{0,1},{1,2},{2,3},{3,4},{4,5},{5,6},{6,7},{7,8},{8,9},{9,10},{10,1... | collective-permute-start | bytes 1769480 | tf_op jit(solution)/shard_map/ppermute | solution.py:18
Sparse Core Ops, SparseCore 0:
  12.9 57.0 all-gather.1
where the time goes:
time: 372 us; the launch traced here: 366 us
  other arithmetic  140 us (38%)
  local copies, waits for them, and re-layouts  85.3 us (23%)
  waiting for transfers between devices  49.8 us (13%)
  loops' own time  41.2 us (11%)
  matrix products  30.6 us (8%)
  between operations  14.2 us (4%)
  starting transfers between devices  4.71 us (1%)
    convert_element_type x16, other arithmetic, kernel_tiles(): kernel.astype(jnp.bfloat16)  131 us
    while x72, local copies, waits for them, and re-layouts  51.5 us
    another operation x1, loops' own time, local(): results = lax.map(one_leaf, (targets, local_near, far_blocks))  41.2 us
    all_gather x1, waiting for transfers between devices, local(): everything = lax.all_gather(payload, 'leaf', axis=0, tiled=True)  31 us
    dot_general x8, matrix products, leaf_product(): jnp.dot(far_flat[coord_count:], far_tiles, preferred_element_type=jnp.flo...  15.1 us
    ppermute x1, waiting for transfers between devices, extended_2(): lax.ppermute(tail, axis, [(i, (i + 1) % count) for i in range(ends)])  13.4 us
    dot_general x8, matrix products, leaf_product(): jnp.dot(near_flat[coord_count:], tiles, preferred_element_type=jnp.float32)  12.2 us
    transpose x8, local copies, waits for them, and re-layouts, leaf_product(): far_flat = far_payload.transpose(1, 0, 2).reshape(far_payload.shape[1], -1)  8.9 us
  transfers between devices with their start and end apart: 3, of which 3 were waited for; matrix products, arithmetic and copies ran while one was open for 1% of the time, Pallas kernels for 0%

commit v1 on v0

v1 whole, which is shorter than its diff:
```python
import functools

import jax
import jax.numpy as jnp
from jax import lax
from jax.experimental import pallas as pl
from jax.experimental.pallas import tpu as pltpu
from jax.sharding import PartitionSpec as P

amplitude = 0.03
length_sq = 4.0
log2_e = 1.4426950408889634
rate = -0.5 / length_sq * log2_e
MIB = 1024 * 1024


def pieces(x):
    high = x.astype(jnp.bfloat16).astype(jnp.float32)
    rest = x - high
    middle = rest.astype(jnp.bfloat16).astype(jnp.float32)
    low = (rest - middle).astype(jnp.bfloat16).astype(jnp.float32)
    return high, middle, low


def norm_rows(coords, first):
    norms = pieces(rate * jnp.sum(coords * coords, axis=0, keepdims=True))
    row = lax.broadcasted_iota(jnp.int32, coords.shape, 0)
    out = jnp.where(row < 6, 1.0, 0.0)
    for at, piece in enumerate(norms):
        out = jnp.where(row == first + at, piece, out)
    return out


def source_factor(coords):
    high, middle, low = pieces(coords * (-2.0 * rate))
    return jnp.concatenate([high, middle, low, norm_rows(coords, 0)], axis=0).astype(jnp.bfloat16)


def target_factor(coords):
    stacked = jnp.concatenate([coords, coords, coords, norm_rows(coords, 3)], axis=0)
    return stacked.T.astype(jnp.bfloat16)


def accumulate(targets, factor, weights):
    exponent = jnp.dot(targets, factor, preferred_element_type=jnp.float32)
    kernel = jnp.exp2(exponent)
    slope = kernel * exponent
    over_sources = (((1,), (1,)), ((), ()))
    return (
        lax.dot_general(kernel.astype(jnp.bfloat16), weights, over_sources, preferred_element_type=jnp.float32),
        lax.dot_general(slope.astype(jnp.bfloat16), weights, over_sources, preferred_element_type=jnp.float32),
    )


def payload_kernel(points_ref, weights_ref, interpolation_ref, skeleton_ref, out_ref):
    leaves, leaf_size, rank = interpolation_ref.shape
    half = rank // 2
    rhs = weights_ref.shape[0]
    dim = points_ref.shape[0]
    for leaf in range(leaves):
        columns = pl.ds(leaf * leaf_size, leaf_size)
        projected = jnp.dot(
            weights_ref[:, columns], interpolation_ref[leaf], preferred_element_type=jnp.float32
        ).astype(jnp.bfloat16)
        position = lax.broadcasted_iota(jnp.int32, (leaf_size, rank), 0)
        selector = jnp.where(position == skeleton_ref[leaf : leaf + 1, :], 1.0, 0.0).astype(jnp.bfloat16)
        chosen = jnp.dot(points_ref[:, columns], selector, preferred_element_type=jnp.float32)
        out_ref[leaf, 0:rhs] = projected[:, :half]
        out_ref[leaf, rhs : 2 * rhs] = projected[:, half:]
        both = jnp.concatenate([chosen[:, :half], chosen[:, half:]], axis=0)
        out_ref[leaf, 2 * rhs : 2 * rhs + 2 * dim] = both.astype(jnp.bfloat16)


def near_kernel(
    lists_ref, points_prev, points_own, points_next, weights_prev, weights_own, weights_next,
    kernel_ref, slope_ref, factor_ref, weight_ref, target_ref, kernel_acc, slope_acc,
):
    leaves, near = lists_ref.shape
    leaf_size = factor_ref.shape[2]
    for side, (points, weights) in enumerate(
        ((points_prev, weights_prev), (points_own, weights_own), (points_next, weights_next))
    ):
        for leaf in range(leaves):
            columns = pl.ds(leaf * leaf_size, leaf_size)
            coords = points[:, columns].astype(jnp.float32)
            factor_ref[side * leaves + leaf] = source_factor(coords)
            weight_ref[side * leaves + leaf] = weights[:, columns]
            if side == 1:
                target_ref[leaf] = target_factor(coords)

    @pl.loop(0, leaves)
    def _(leaf):
        kernel_acc[...] = jnp.zeros_like(kernel_acc)
        slope_acc[...] = jnp.zeros_like(slope_acc)

        @pl.loop(0, near)
        def _(slot):
            source = lists_ref[leaf, slot]
            kernel, slope = accumulate(target_ref[leaf], factor_ref[source], weight_ref[source])
            kernel_acc[...] += kernel
            slope_acc[...] += slope

        columns = pl.ds(pl.multiple_of(leaf * leaf_size, leaf_size), leaf_size)
        kernel_ref[:, columns] = kernel_acc[...].T
        slope_ref[:, columns] = slope_acc[...].T


def far_kernel(
    lists_ref, points_ref, near_kernel_ref, near_slope_ref, everything_ref,
    kernel_ref, slope_ref, block_ref, kernel_acc, slope_acc, semaphore,
):
    leaves, far = lists_ref.shape
    leaf_size = points_ref.shape[1] // leaves
    rows = block_ref.shape[2]
    dim = points_ref.shape[0]
    rhs = kernel_ref.shape[0]

    def fetch(leaf, slot):
        return pltpu.make_async_copy(
            everything_ref.at[lists_ref[leaf, slot]], block_ref.at[leaf, slot], semaphore.at[leaf, slot]
        )

    @pl.loop(0, leaves)
    def _(leaf):
        @pl.loop(0, far)
        def _(slot):
            fetch(leaf, slot).start()

    @pl.loop(0, leaves)
    def _(leaf):
        columns = pl.ds(pl.multiple_of(leaf * leaf_size, leaf_size), leaf_size)
        targets = target_factor(points_ref[:, columns].astype(jnp.float32))
        kernel_acc[...] = jnp.zeros_like(kernel_acc)
        slope_acc[...] = jnp.zeros_like(slope_acc)

        @pl.loop(0, far // 2)
        def _(pair):
            halves = []
            coords = []
            for member in range(2):
                slot = pair * 2 + member
                fetch(leaf, slot).wait()
                for part in range(2):
                    halves.append(block_ref[leaf, slot, part * rhs : (part + 1) * rhs])
                both = block_ref[leaf, slot, 2 * rhs : rows].astype(jnp.float32)
                coords += [both[:dim], both[dim:]]
            factor = source_factor(jnp.concatenate(coords, axis=1))
            kernel, slope = accumulate(targets, factor, jnp.concatenate(halves, axis=1))
            kernel_acc[...] += kernel
            slope_acc[...] += slope

        kernel_ref[:, columns] = amplitude * (near_kernel_ref[:, columns] + kernel_acc[...].T)
        slope_ref[:, columns] = (amplitude / (length_sq * rate)) * (near_slope_ref[:, columns] + slope_acc[...].T)


def local(points, weights, interpolation, skeleton, near_lists, far_lists):
    position = lax.axis_index("leaf")
    count = lax.axis_size("leaf")
    leaves, leaf_size, rank = interpolation.shape
    dim, rhs = points.shape[0], weights.shape[0]
    far, near = far_lists.shape[1], near_lists.shape[1]
    width = points.shape[1]
    vmem = pl.BlockSpec(memory_space=pltpu.VMEM)
    smem = pl.BlockSpec(memory_space=pltpu.SMEM)
    up = [(i, i + 1) for i in range(count - 1)]
    down = [(i + 1, i) for i in range(count - 1)]
    points_prev, weights_prev = lax.ppermute(points, "leaf", up), lax.ppermute(weights, "leaf", up)
    points_next, weights_next = lax.ppermute(points, "leaf", down), lax.ppermute(weights, "leaf", down)

    rows = 2 * (rhs + dim)
    payload = pl.pallas_call(
        payload_kernel,
        out_shape=jax.ShapeDtypeStruct((leaves, rows, rank // 2), jnp.bfloat16),
        in_specs=[vmem] * 4,
        out_specs=vmem,
        compiler_params=pltpu.CompilerParams(vmem_limit_bytes=32 * MIB),
        cost_estimate=pl.CostEstimate(
            flops=2 * leaves * (rhs + dim) * leaf_size * rank, bytes_accessed=interpolation.size * 2, transcendentals=0
        ),
    )(points, weights, interpolation, skeleton)
    everything = lax.all_gather(payload, "leaf", axis=0, tiled=True)

    def cost(sources):
        pairs = leaves * leaf_size * sources
        return pl.CostEstimate(
            flops=pairs * 2 * (256 + 512), bytes_accessed=6 * rhs * width * 2, transcendentals=pairs
        )

    partial = jax.ShapeDtypeStruct((rhs, width), jnp.float32)
    accumulator = pltpu.VMEM((leaf_size, rhs), jnp.float32)
    local_near = near_lists - (position - 1) * leaves
    near_kernel_part, near_slope_part = pl.pallas_call(
        near_kernel,
        out_shape=(partial, partial),
        in_specs=[smem] + [vmem] * 6,
        out_specs=(vmem, vmem),
        scratch_shapes=[
            pltpu.VMEM((3 * leaves, 4 * dim, leaf_size), jnp.bfloat16),
            pltpu.VMEM((3 * leaves, rhs, leaf_size), jnp.bfloat16),
            pltpu.VMEM((leaves, leaf_size, 4 * dim), jnp.bfloat16),
            accumulator,
            accumulator,
        ],
        compiler_params=pltpu.CompilerParams(vmem_limit_bytes=48 * MIB),
        cost_estimate=cost(near * leaf_size),
    )(local_near, points_prev, points, points_next, weights_prev, weights, weights_next)

    return pl.pallas_call(
        far_kernel,
        out_shape=(partial, partial),
        in_specs=[smem, vmem, vmem, vmem, pl.BlockSpec(memory_space=pl.ANY)],
        out_specs=(vmem, vmem),
        scratch_shapes=[
            pltpu.VMEM((leaves, far, rows, rank // 2), jnp.bfloat16),
            accumulator,
            accumulator,
            pltpu.SemaphoreType.DMA((leaves, far)),
        ],
        compiler_params=pltpu.CompilerParams(vmem_limit_bytes=48 * MIB),
        cost_estimate=cost(far * rank),
    )(far_lists, points, near_kernel_part, near_slope_part, everything)


def solution(mesh):
    placed = (
        P(None, ("groups", "leaf")),
        P(None, ("groups", "leaf")),
        P(("groups", "leaf"), None, None),
        P(("groups", "leaf"), None),
        P(("groups", "leaf"), None),
        P(("groups", "leaf"), None),
    )
    return jax.shard_map(
        local,
        mesh=mesh,
        in_specs=placed,
        out_specs=(P(None, ("groups", "leaf")), P(None, ("groups", "leaf"))),
        check_vma=False,
    )
```

time: 372 us -> 117 us (0.31); the launches traced: 366 us -> 117 us
  other arithmetic: 140 us -> 0.7 us
  local copies, waits for them, and re-layouts: 85.3 us -> 6.05 us
  Pallas kernels: 0 us -> 73 us
  loops' own time: 41.2 us -> 0 us
  waiting for transfers between devices: 49.8 us -> 11.9 us
  matrix products: 30.6 us -> 0 us
  starting transfers between devices: 4.71 us -> 11.2 us
    convert_element_type x40 -> x0, other arithmetic: 132 us -> none  [the longest x16 131 us: kernel_tiles(): kernel.astype(jnp.bfloat16)]
    pallas_call x0 -> x3, Pallas kernels: none -> 73 us  [the longest x1 38 us: local(): pl.pallas_call(near_kernel, out_shape=(partial, partial), in_specs=[smem]...]
    while x72 -> x0, local copies, waits for them, and re-layouts: 51.5 us -> none
    another operation x1 -> x0, loops' own time: 41.2 us -> none  [local(): results = lax.map(one_leaf, (targets, local_near, far_blocks))]
    all_gather x1, waiting for transfers between devices: 31 us -> 0.02 us  [local(): everything = lax.all_gather(payload, 'leaf', axis=0, tiled=True)]
    dot_general x18 -> x0, matrix products: 30.6 us -> none  [the longest x8 15.1 us: leaf_product(): jnp.dot(far_flat[coord_count:], far_tiles, preferred_element_type=jnp.flo...]
    transpose x8 -> x0, local copies, waits for them, and re-layouts: 8.9 us -> none  [leaf_product(): far_flat = far_payload.transpose(1, 0, 2).reshape(far_payload.shape[1], -1)]
    another operation x8 -> x0, local copies, waits for them, and re-layouts: 7.16 us -> none  [one_leaf(): near_blocks = jnp.stack(pieces, axis=1)]
  transfers between devices with their start and end apart: 3 -> 5, of which waited for: 3 -> 2; matrix products, arithmetic and copies ran while one was open for 1% -> 1% of each run, Pallas kernels for 0% -> 32%
where the time goes in v1:
time: 117 us
  Pallas kernels  73 us (62%)
  between operations  14.1 us (12%)
  waiting for transfers between devices  11.9 us (10%)
  starting transfers between devices  11.2 us (10%)
  local copies, waits for them, and re-layouts  6.05 us (5%)
    pallas_call x1, Pallas kernels, local(): pl.pallas_call(near_kernel, out_shape=(partial, partial), in_specs=[smem]...  38 us
    pallas_call x1, Pallas kernels, local(): pl.pallas_call(far_kernel, out_shape=(partial, partial), in_specs=[smem,...  33.5 us
    ppermute x1, waiting for transfers between devices, local(): lax.ppermute(points, 'leaf', up)  10.6 us
    unnamed x16, local copies, waits for them, and re-layouts  6.05 us
    ppermute x1, starting transfers between devices, local(): lax.ppermute(points, 'leaf', down)  4.54 us
    ppermute x1, starting transfers between devices, local(): lax.ppermute(weights, 'leaf', down)  2.76 us
  transfers between devices with their start and end apart: 5, of which 2 were waited for; matrix products, arithmetic and copies ran while one was open for 1% of the time, Pallas kernels for 32%

profile of v1, /device:TPU:16, one launch (start us, length us, event | category | flops | bytes accessed | tf_op | source)
XLA Modules:
  0.0 116.9 jit_solution(10040579031380961168)
XLA Ops:
  7.2 0.0 all-gather.2.cloned.1.call-start
  7.2 0.0 copy-start
  7.2 1.6 %copy-done = bf16[8,512,256]{2,1,0:T(8,128)(2,1)S(1)} copy-done((bf16[8,512,256]{2,1,0:T(8,128)(2,1)S(1)}, bf16[8,512,256]{2,1,0:T(8,128)(2,1)}, u32[]{:S(2)}) %copy-start) | copy-done | bytes 2097176
  8.8 0.0 copy-start.1
  8.8 1.0 copy-done.1
  9.8 0.0 copy-start.3
  9.8 0.8 copy-done.3
  10.7 0.0 copy-start.6
  10.7 0.7 copy-done.6
  11.4 1.5 %shard_map.78 = bf16[8,144,128]{2,1,0:T(8,128)(2,1)} custom-call(bf16[8,4096]{1,0:T(8,128)(2,1)S(1)} %copy-done.3, bf16[64,4096]{1,0:T(8,128)(2,1)S(1)} %copy-done.1, bf16[8,512,256]{2,1,0:T(8,128)(2,1)S(1)} %copy-done, s32[8,256]{1,0:T(8,128)S(1)} %copy-done.6), custom_call_target="tpu_custom_call" | custom-call | flops 150994944 | bytes 2097152 | tf_op jit(solution)/shard_map/pallas_call | solution.py:171
  12.9 0.0 all-gather.2.cloned.1.call-update
  12.9 2.8 %collective-permute-start.3 = (bf16[64,4096]{1,0:T(8,128)(2,1)}, bf16[64,4096]{1,0:T(8,128)(2,1)S(1)}, u32[]{:S(2)}, u32[]{:S(2)}) collective-permute-start(bf16[64,4096]{1,0:T(8,128)(2,1)} %weights_ref.1), channel_id=1, source_target_pairs={{1,0},{2,1},{3,2},{4,3},{5,4},{6,5},{7,6},{8,7},{9,8},{10,9},{11,1... | collective-permute-start | bytes 1572872 | tf_op jit(solution)/shard_map/ppermute | solution.py:168
  15.7 1.9 %collective-permute-start.2 = (bf16[64,4096]{1,0:T(8,128)(2,1)}, bf16[64,4096]{1,0:T(8,128)(2,1)S(1)}, u32[]{:S(2)}, u32[]{:S(2)}) collective-permute-start(bf16[64,4096]{1,0:T(8,128)(2,1)} %weights_ref.1), channel_id=1, source_target_pairs={{0,1},{1,2},{2,3},{3,4},{4,5},{5,6},{6,7},{7,8},{8,9},{9,10},{10,1... | collective-permute-start | bytes 1572872 | tf_op jit(solution)/shard_map/ppermute | solution.py:167
  17.6 4.5 %collective-permute-start.1 = (bf16[8,4096]{1,0:T(8,128)(2,1)}, bf16[8,4096]{1,0:T(8,128)(2,1)S(1)}, u32[]{:S(2)}, u32[]{:S(2)}) collective-permute-start(bf16[8,4096]{1,0:T(8,128)(2,1)} %points_ref.3), channel_id=1, source_target_pairs={{1,0},{2,1},{3,2},{4,3},{5,4},{6,5},{7,6},{8,7},{9,8},{10,9},{11,1... | collective-permute-start | bytes 196616 | tf_op jit(solution)/shard_map/ppermute | solution.py:168
  22.2 1.9 %collective-permute-start = (bf16[8,4096]{1,0:T(8,128)(2,1)}, bf16[8,4096]{1,0:T(8,128)(2,1)S(1)}, u32[]{:S(2)}, u32[]{:S(2)}) collective-permute-start(bf16[8,4096]{1,0:T(8,128)(2,1)} %points_ref.3), channel_id=1, source_target_pairs={{0,1},{1,2},{2,3},{3,4},{4,5},{5,6},{6,7},{7,8},{8,9},{9,10},{10,1... | collective-permute-start | bytes 196616 | tf_op jit(solution)/shard_map/ppermute | solution.py:167
  24.1 0.0 copy-start.7
  24.1 0.7 broadcast_subtract_fusion.lists_ref
  24.8 1.3 %collective-permute-done.1.points_next = bf16[8,4096]{1,0:T(8,128)(2,1)S(1)} collective-permute-done((bf16[8,4096]{1,0:T(8,128)(2,1)}, bf16[8,4096]{1,0:T(8,128)(2,1)S(1)}, u32[]{:S(2)}, u32[]{:S(2)}) %collective-permute-start.1) | collective-permute-done | bytes 65568 | tf_op jit(solution)/shard_map/ppermute | solution.py:168
  26.1 10.6 %collective-permute-done.points_prev = bf16[8,4096]{1,0:T(8,128)(2,1)S(1)} collective-permute-done((bf16[8,4096]{1,0:T(8,128)(2,1)}, bf16[8,4096]{1,0:T(8,128)(2,1)S(1)}, u32[]{:S(2)}, u32[]{:S(2)}) %collective-permute-start) | collective-permute-done | bytes 65568 | tf_op jit(solution)/shard_map/ppermute | solution.py:167
  36.6 0.0 collective-permute-done.3.weights_next
  36.6 0.0 collective-permute-done.2.weights_prev
  36.6 0.0 copy-start.2
  36.7 1.0 copy-done.2
  37.7 0.0 copy-start.4
  37.7 0.8 copy-done.4
  38.5 0.0 copy-start.5
  38.5 38.0 %shard_map.77 = (f32[64,4096]{1,0:T(8,128)S(1)}, f32[64,4096]{1,0:T(8,128)S(1)}) custom-call(s32[8,8]{1,0:T(8,128)S(1)} %broadcast_subtract_fusion.lists_ref, bf16[8,4096]{1,0:T(8,128)(2,1)S(1)} %collective-permute-done.points_prev, bf16[8,4096]{1,0:T(8,128)(2,1)S(1)} %copy-done.4, bf16[8,4096]{1,0:T(8,128)(2,1)S(1)} %collective-permute-done.1.points_next, ...), custom_call_target="tpu_custom_call" | custom-call | flops 25769803776 | bytes 3145728 | tf_op jit(solution)/shard_map/pallas_call | solution.py:192
  76.5 0.0 all-gather.2.cloned.1.call-done.everything_ref
  76.6 0.0 copy-done.7
  76.6 0.0 copy-done.5
  76.6 33.5 %shard_map.79 = (f32[64,4096]{1,0:T(8,128)}, f32[64,4096]{1,0:T(8,128)}) custom-call(s32[8,12]{1,0:T(8,128)S(1)} %copy-done.7, bf16[8,4096]{1,0:T(8,128)(2,1)S(1)} %copy-done.5, f32[64,4096]{1,0:T(8,128)S(1)} %get-tuple-element.4.near_kernel_ref, f32[64,4096]{1,0:T(8,128)S(1)} %get-tuple-element.5.near_slope_ref, ...), custom_call_target="tpu_custom_call" | custom-call | flops 19327352832 | bytes 3145728 | tf_op jit(solution)/shard_map/pallas_call | solution.py:208
Async XLA Ops:
  7.2 69.4 %all-gather.2.cloned.1.call-start = ((), (), s32[]{:S(2)}) async-start(), calls=%async_computation | async-start | bytes 5013504 | tf_op jit(solution)/shard_map/all_gather | solution.py:181
  7.2 1.6 %copy-start = (bf16[8,512,256]{2,1,0:T(8,128)(2,1)S(1)}, bf16[8,512,256]{2,1,0:T(8,128)(2,1)}, u32[]{:S(2)}) copy-start(bf16[8,512,256]{2,1,0:T(8,128)(2,1)} %interpolation_ref.1) | copy-start | bytes 6291460
  8.8 1.0 copy-start.1
  9.8 0.8 copy-start.3
  10.7 0.7 copy-start.6
  12.9 23.7 %collective-permute-start.3 = (bf16[64,4096]{1,0:T(8,128)(2,1)}, bf16[64,4096]{1,0:T(8,128)(2,1)S(1)}, u32[]{:S(2)}, u32[]{:S(2)}) collective-permute-start(bf16[64,4096]{1,0:T(8,128)(2,1)} %weights_ref.1), channel_id=1, source_target_pairs={{1,0},{2,1},{3,2},{4,3},{5,4},{6,5},{7,6},{8,7},{9,8},{10,9},{11,1... | collective-permute-start | bytes 1572872 | tf_op jit(solution)/shard_map/ppermute | solution.py:168
  15.7 21.0 %collective-permute-start.2 = (bf16[64,4096]{1,0:T(8,128)(2,1)}, bf16[64,4096]{1,0:T(8,128)(2,1)S(1)}, u32[]{:S(2)}, u32[]{:S(2)}) collective-permute-start(bf16[64,4096]{1,0:T(8,128)(2,1)} %weights_ref.1), channel_id=1, source_target_pairs={{0,1},{1,2},{2,3},{3,4},{4,5},{5,6},{6,7},{7,8},{8,9},{9,10},{10,1... | collective-permute-start | bytes 1572872 | tf_op jit(solution)/shard_map/ppermute | solution.py:167
  17.6 8.5 %collective-permute-start.1 = (bf16[8,4096]{1,0:T(8,128)(2,1)}, bf16[8,4096]{1,0:T(8,128)(2,1)S(1)}, u32[]{:S(2)}, u32[]{:S(2)}) collective-permute-start(bf16[8,4096]{1,0:T(8,128)(2,1)} %points_ref.3), channel_id=1, source_target_pairs={{1,0},{2,1},{3,2},{4,3},{5,4},{6,5},{7,6},{8,7},{9,8},{10,9},{11,1... | collective-permute-start | bytes 196616 | tf_op jit(solution)/shard_map/ppermute | solution.py:168
  22.2 14.5 %collective-permute-start = (bf16[8,4096]{1,0:T(8,128)(2,1)}, bf16[8,4096]{1,0:T(8,128)(2,1)S(1)}, u32[]{:S(2)}, u32[]{:S(2)}) collective-permute-start(bf16[8,4096]{1,0:T(8,128)(2,1)} %points_ref.3), channel_id=1, source_target_pairs={{0,1},{1,2},{2,3},{3,4},{4,5},{5,6},{6,7},{7,8},{8,9},{9,10},{10,1... | collective-permute-start | bytes 196616 | tf_op jit(solution)/shard_map/ppermute | solution.py:167
  24.1 52.5 %copy-start.7 = (s32[8,12]{1,0:T(8,128)S(1)}, s32[8,12]{1,0:T(8,128)}, u32[]{:S(2)}) copy-start(s32[8,12]{1,0:T(8,128)} %lists_ref.1) | copy-start | bytes 1156
  36.6 1.0 copy-start.2
  37.7 0.8 copy-start.4
  38.5 38.0 %copy-start.5 = (bf16[8,4096]{1,0:T(8,128)(2,1)S(1)}, bf16[8,4096]{1,0:T(8,128)(2,1)}, u32[]{:S(2)}) copy-start(bf16[8,4096]{1,0:T(8,128)(2,1)} %points_ref.3) | copy-start | bytes 196612
Sparse Core Ops, SparseCore 0:
  13.0 57.1 all-gather.1

commit v2 on v1

--- a/solution.py
+++ b/solution.py
@@ -52,7 +52,7 @@
     )
 
 
-def payload_kernel(points_ref, weights_ref, interpolation_ref, skeleton_ref, out_ref):
+def skeleton_block(points_ref, weights_ref, interpolation_ref, skeleton_ref, out_ref):
     leaves, leaf_size, rank = interpolation_ref.shape
     half = rank // 2
     rhs = weights_ref.shape[0]
@@ -72,37 +72,233 @@
 
 
 def near_kernel(
-    lists_ref, points_prev, points_own, points_next, weights_prev, weights_own, weights_next,
-    kernel_ref, slope_ref, factor_ref, weight_ref, target_ref, kernel_acc, slope_acc,
+    count, lists_ref, points_ref, weights_ref, interpolation_ref, skeleton_ref,
+    kernel_ref, slope_ref, all_ref,
+    factor_ref, weight_ref, target_ref, kernel_acc, slope_acc,
+    payload_ref, packed_ref, halo_points, halo_weights,
+    own_sem, halo_send, halo_recv, up_send, up_recv, down_send, down_recv,
+    across_send, across_recv, core_send, core_recv,
 ):
     leaves, near = lists_ref.shape
     leaf_size = factor_ref.shape[2]
-    for side, (points, weights) in enumerate(
-        ((points_prev, weights_prev), (points_own, weights_own), (points_next, weights_next))
-    ):
-        for leaf in range(leaves):
-            columns = pl.ds(leaf * leaf_size, leaf_size)
-            coords = points[:, columns].astype(jnp.float32)
-            factor_ref[side * leaves + leaf] = source_factor(coords)
-            weight_ref[side * leaves + leaf] = weights[:, columns]
-            if side == 1:
-                target_ref[leaf] = target_factor(coords)
+    dim = points_ref.shape[0]
+    middle = packed_ref.shape[1]
+    me = lax.axis_index("leaf")
+    length = count // 4
+    place, lane = me // 4, lax.rem(me, 4)
+    row, core = lane // 2, lax.rem(lane, 2)
+    across = place * 4 + (1 - row) * 2 + core
+    sibling = place * 4 + row * 2 + (1 - core)
+    has_prev, has_next = me > 0, me < count - 1
+    has_low, has_high = place > 0, place < length - 1
+
+    def remote(source, target, send, recv, device):
+        return pltpu.make_async_remote_copy(
+            src_ref=source, dst_ref=target, send_sem=send, recv_sem=recv,
+            device_id={"leaf": device}, device_id_type=pl.DeviceIdType.MESH,
+        )
+
+    barrier = pltpu.get_barrier_semaphore()
+
+    def greet(device):
+        pl.semaphore_signal(barrier, inc=1, device_id={"leaf": device}, device_id_type=pl.DeviceIdType.MESH)
+
+    greet(across)
+    greet(sibling)
+    others = (
+        (jnp.logical_and(has_prev, core == 0), me - 1), (jnp.logical_and(has_next, core == 1), me + 1),
+        (has_low, me - 4), (has_high, me + 4),
+    )
+    peers = 2
+    for present, device in others:
+        peers = peers + present.astype(jnp.int32)
+
+        @pl.when(present)
+        def _(device=device):
+            greet(device)
+
+    packed_ref[...] = jnp.concatenate(
+        [points_ref[:, :middle].astype(jnp.float32), points_ref[:, middle:].astype(jnp.float32)], axis=0
+    ).astype(jnp.bfloat16)
+    pl.semaphore_wait(barrier, peers)
+
+    def halo(side, device):
+        return (
+            remote(packed_ref, halo_points.at[side], halo_send.at[side, 0], halo_recv.at[side, 0], device),
+            remote(weights_ref, halo_weights.at[side], halo_send.at[side, 1], halo_recv.at[side, 1], device),
+        )
+
+    to_next, to_prev = halo(0, me + 1), halo(1, me - 1)
+    for present, copies in ((has_next, to_next), (has_prev, to_prev)):
+
+        @pl.when(present)
+        def _(copies=copies):
+            for copy in copies:
+                copy.start()
+
+    for present, side in ((has_prev, 0), (has_next, 1)):
+
+        @pl.when(jnp.logical_not(present))
+        def _(side=side):
+            halo_points[side] = jnp.zeros_like(halo_points[side])
+            halo_weights[side] = jnp.zeros_like(halo_weights[side])
+
+    skeleton_block(points_ref, weights_ref, interpolation_ref, skeleton_ref, payload_ref)
+
+    def slot(place_of, lane_of):
+        return all_ref.at[pl.ds((place_of * 4 + lane_of) * leaves, leaves)]
+
+    def up(step):
+        source = payload_ref if step == 0 else slot(place - step, lane)
+        return remote(source, slot(place - step, lane), up_send.at[step], up_recv.at[step + 1], me + 4)
+
+    def down(step):
+        source = payload_ref if step == 0 else slot(place + step, lane)
+        return remote(source, slot(place + step, lane), down_send.at[step], down_recv.at[step + 1], me - 4)
+
+    def over(place_of, source=None):
+        block = slot(place_of, lane)
+        return remote(
+            block if source is None else source, block, across_send.at[place_of], across_recv.at[place_of], across
+        )
+
+    def share(place_of, row_of, source=None):
+        block = slot(place_of, row_of * 2 + core)
+        return remote(
+            block if source is None else source, block,
+            core_send.at[place_of, row_of], core_recv.at[place_of, row_of], sibling,
+        )
+
+    own = pltpu.make_async_copy(payload_ref, slot(place, lane), own_sem)
+    own.start()
+    over(place, payload_ref).start()
+    share(place, row, payload_ref).start()
+    for present, first in ((has_high, up(0)), (has_low, down(0))):
+
+        @pl.when(present)
+        def _(first=first):
+            first.start()
+
+    def arrived_along(step):
+        @pl.when(place - step >= 0)
+        def _():
+            remote(payload_ref, slot(place - step, lane), up_send.at[0], up_recv.at[step], me + 4).wait_recv()
+
+            @pl.when(has_high)
+            def _():
+                up(step).start()
+
+            over(place - step).start()
+            share(place - step, row).start()
+
+        @pl.when(place + step < length)
+        def _():
+            remote(payload_ref, slot(place + step, lane), down_send.at[0], down_recv.at[step], me - 4).wait_recv()
+
+            @pl.when(has_low)
+            def _():
+                down(step).start()
+
+            over(place + step).start()
+            share(place + step, row).start()
+
+    def arrived_across(step):
+        def one(place_of):
+            remote(
+                payload_ref, slot(place_of, (1 - row) * 2 + core), across_send.at[place_of],
+                across_recv.at[place_of], across,
+            ).wait_recv()
+            share(place_of, 1 - row).start()
+
+        if step == 0:
+            one(place)
+            return
+
+        @pl.when(place - step >= 0)
+        def _():
+            one(place - step)
+
+        @pl.when(place + step < length)
+        def _():
+            one(place + step)
 
     @pl.loop(0, leaves)
     def _(leaf):
-        kernel_acc[...] = jnp.zeros_like(kernel_acc)
-        slope_acc[...] = jnp.zeros_like(slope_acc)
-
-        @pl.loop(0, near)
-        def _(slot):
-            source = lists_ref[leaf, slot]
-            kernel, slope = accumulate(target_ref[leaf], factor_ref[source], weight_ref[source])
-            kernel_acc[...] += kernel
-            slope_acc[...] += slope
-
         columns = pl.ds(pl.multiple_of(leaf * leaf_size, leaf_size), leaf_size)
-        kernel_ref[:, columns] = kernel_acc[...].T
-        slope_ref[:, columns] = slope_acc[...].T
+        coords = points_ref[:, columns].astype(jnp.float32)
+        factor_ref[leaves + leaf] = source_factor(coords)
+        weight_ref[leaves + leaf] = weights_ref[:, columns]
+        target_ref[leaf] = target_factor(coords)
+        kernel, slope = accumulate(target_ref[leaf], factor_ref[leaves + leaf], weight_ref[leaves + leaf])
+        kernel_acc[leaf] = kernel
+        slope_acc[leaf] = slope
+
+    for present, copies in ((has_prev, halo(0, me + 1)), (has_next, halo(1, me - 1))):
+
+        @pl.when(present)
+        def _(copies=copies):
+            for copy in copies:
+                copy.wait_recv()
+
+    for side in range(2):
+        for leaf in range(leaves):
+            begin = leaf * leaf_size
+            part, begin_in = begin // middle, begin % middle
+            both = halo_points[side, :, begin_in : begin_in + leaf_size].astype(jnp.float32)
+            coords = both[part * dim : (part + 1) * dim]
+            factor_ref[2 * leaves * side + leaf] = source_factor(coords)
+            weight_ref[2 * leaves * side + leaf] = halo_weights[side, :, begin : begin + leaf_size]
+
+    def run_leaves(first, last):
+        @pl.loop(first, last)
+        def _(leaf):
+            @pl.loop(1, near)
+            def _(entry):
+                source = lists_ref[leaf, entry]
+                kernel, slope = accumulate(target_ref[leaf], factor_ref[source], weight_ref[source])
+                kernel_acc[leaf] += kernel
+                slope_acc[leaf] += slope
+
+            columns = pl.ds(pl.multiple_of(leaf * leaf_size, leaf_size), leaf_size)
+            kernel_ref[:, columns] = kernel_acc[leaf].T
+            slope_ref[:, columns] = slope_acc[leaf].T
+
+    done = 0
+    for step in range(1, length):
+        upto = min(leaves - 1, max(done, step * (leaves - 1) // length + 1))
+        if upto > done:
+            run_leaves(done, upto)
+            done = upto
+        arrived_along(step)
+        arrived_across(step - 1)
+    run_leaves(done, leaves)
+    arrived_across(length - 1)
+
+    own.wait()
+    for present, copies in ((has_next, to_next), (has_prev, to_prev)):
+
+        @pl.when(present)
+        def _(copies=copies):
+            for copy in copies:
+                copy.wait_send()
+
+    for step in range(length):
+        for present, there, copy in (
+            (has_high, place - step >= 0, up(step)), (has_low, place + step < length, down(step)),
+        ):
+
+            @pl.when(jnp.logical_and(present, there))
+            def _(copy=copy):
+                copy.wait_send()
+
+    for place_of in range(length):
+        over(place_of).wait_send()
+        for row_of in range(2):
+            share(place_of, row_of).wait_send()
+            remote(
+                payload_ref, slot(place_of, row_of * 2 + 1 - core), core_send.at[place_of, row_of],
+                core_recv.at[place_of, row_of], sibling,
+            ).wait_recv()
 
 
 def far_kernel(
@@ -162,23 +358,7 @@
     width = points.shape[1]
     vmem = pl.BlockSpec(memory_space=pltpu.VMEM)
     smem = pl.BlockSpec(memory_space=pltpu.SMEM)
-    up = [(i, i + 1) for i in range(count - 1)]
-    down = [(i + 1, i) for i in range(count - 1)]
-    points_prev, weights_prev = lax.ppermute(points, "leaf", up), lax.ppermute(weights, "leaf", up)
-    points_next, weights_next = lax.ppermute(points, "leaf", down), lax.ppermute(weights, "leaf", down)
-
     rows = 2 * (rhs + dim)
-    payload = pl.pallas_call(
-        payload_kernel,
-        out_shape=jax.ShapeDtypeStruct((leaves, rows, rank // 2), jnp.bfloat16),
-        in_specs=[vmem] * 4,
-        out_specs=vmem,
-        compiler_params=pltpu.CompilerParams(vmem_limit_bytes=32 * MIB),
-        cost_estimate=pl.CostEstimate(
-            flops=2 * leaves * (rhs + dim) * leaf_size * rank, bytes_accessed=interpolation.size * 2, transcendentals=0
-        ),
-    )(points, weights, interpolation, skeleton)
-    everything = lax.all_gather(payload, "leaf", axis=0, tiled=True)
 
     def cost(sources):
         pairs = leaves * leaf_size * sources
@@ -189,21 +369,34 @@
     partial = jax.ShapeDtypeStruct((rhs, width), jnp.float32)
     accumulator = pltpu.VMEM((leaf_size, rhs), jnp.float32)
     local_near = near_lists - (position - 1) * leaves
-    near_kernel_part, near_slope_part = pl.pallas_call(
-        near_kernel,
-        out_shape=(partial, partial),
-        in_specs=[smem] + [vmem] * 6,
-        out_specs=(vmem, vmem),
+    dma = pltpu.SemaphoreType.DMA
+    length = count // 4
+    near_kernel_part, near_slope_part, everything = pl.pallas_call(
+        functools.partial(near_kernel, count),
+        out_shape=(partial, partial, jax.ShapeDtypeStruct((count * leaves, rows, rank // 2), jnp.bfloat16)),
+        in_specs=[smem] + [vmem] * 4,
+        out_specs=(vmem, vmem, pl.BlockSpec(memory_space=pl.ANY)),
         scratch_shapes=[
             pltpu.VMEM((3 * leaves, 4 * dim, leaf_size), jnp.bfloat16),
             pltpu.VMEM((3 * leaves, rhs, leaf_size), jnp.bfloat16),
             pltpu.VMEM((leaves, leaf_size, 4 * dim), jnp.bfloat16),
-            accumulator,
-            accumulator,
+            pltpu.VMEM((leaves, leaf_size, rhs), jnp.float32),
+            pltpu.VMEM((leaves, leaf_size, rhs), jnp.float32),
+            pltpu.VMEM((leaves, rows, rank // 2), jnp.bfloat16),
+            pltpu.VMEM((2 * dim, width // 2), jnp.bfloat16),
+            pltpu.VMEM((2, 2 * dim, width // 2), jnp.bfloat16),
+            pltpu.VMEM((2, rhs, width), jnp.bfloat16),
+            dma(()),
+            dma((2, 2)), dma((2, 2)),
+            dma((length + 1,)), dma((length + 1,)), dma((length + 1,)), dma((length + 1,)),
+            dma((length,)), dma((length,)),
+            dma((length, 2)), dma((length, 2)),
         ],
-        compiler_params=pltpu.CompilerParams(vmem_limit_bytes=48 * MIB),
+        compiler_params=pltpu.CompilerParams(
+            collective_id=0, has_side_effects=True, vmem_limit_bytes=48 * MIB
+        ),
         cost_estimate=cost(near * leaf_size),
-    )(local_near, points_prev, points, points_next, weights_prev, weights, weights_next)
+    )(local_near, points, weights, interpolation, skeleton)
 
     return pl.pallas_call(
         far_kernel,

time: 117 us -> 97.5 us (0.83)
  Pallas kernels: 73 us -> 91.6 us
  between operations: 14.1 us -> 0.66 us
  waiting for transfers between devices: 11.9 us -> 0 us
  starting transfers between devices: 11.2 us -> 0 us
  local copies, waits for them, and re-layouts: 6.05 us -> 4.17 us
    pallas_call x2 -> x1, Pallas kernels: 39.5 us -> 58.1 us  [local(): pl.pallas_call(functools.partial(near_kernel, count), out_shape=(partial,...]
    ppermute x4 -> x0, waiting for transfers between devices: 11.9 us -> none  [the longest x1 10.6 us: local(): lax.ppermute(points, 'leaf', up)]
    ppermute x4 -> x0, starting transfers between devices: 11.1 us -> none  [the longest x1 4.54 us: local(): lax.ppermute(points, 'leaf', down)]
    unnamed x16 -> x12, local copies, waits for them, and re-layouts: 6.05 us -> 4.17 us
  transfers between devices with their start and end apart: 5 -> 0, of which waited for: 2 -> 0; matrix products, arithmetic and copies ran while one was open for 1% -> 0% of each run, Pallas kernels for 32% -> 0%
where the time goes in v2:
time: 97.5 us; the launch traced here: 97.1 us
  Pallas kernels  91.6 us (94%)
  local copies, waits for them, and re-layouts  4.17 us (4%)
    pallas_call x1, Pallas kernels, local(): pl.pallas_call(functools.partial(near_kernel, count), out_shape=(partial,...  58.1 us
    pallas_call x1, Pallas kernels, local(): pl.pallas_call(far_kernel, out_shape=(partial, partial), in_specs=[smem,...  33.5 us
    unnamed x12, local copies, waits for them, and re-layouts  4.17 us

profile of v2, /device:TPU:16, one launch (start us, length us, event | category | flops | bytes accessed | tf_op | source)
XLA Modules:
  0.0 97.1 jit_solution(7698618291839450187)
XLA Ops:
  0.6 0.7 broadcast_subtract_fusion.lists_ref
  1.3 0.0 copy-start
  1.3 1.6 %copy-done = bf16[8,512,256]{2,1,0:T(8,128)(2,1)S(1)} copy-done((bf16[8,512,256]{2,1,0:T(8,128)(2,1)S(1)}, bf16[8,512,256]{2,1,0:T(8,128)(2,1)}, u32[]{:S(2)}) %copy-start) | copy-done | bytes 2097176
  2.9 0.0 copy-start.1
  2.9 1.0 %copy-done.1 = bf16[64,4096]{1,0:T(8,128)(2,1)S(1)} copy-done((bf16[64,4096]{1,0:T(8,128)(2,1)S(1)}, bf16[64,4096]{1,0:T(8,128)(2,1)}, u32[]{:S(2)}) %copy-start.1) | copy-done | bytes 524312
  4.0 0.0 copy-start.2
  4.0 0.8 copy-done.2
  4.8 0.0 copy-start.4
  4.8 0.7 copy-done.4
  5.5 0.0 copy-start.3
  5.5 0.0 copy-start.5
  5.5 58.1 %shard_map.77 = (f32[64,4096]{1,0:T(8,128)S(1)}, f32[64,4096]{1,0:T(8,128)S(1)}, bf16[128,144,128]{2,1,0:T(8,128)(2,1)}) custom-call(s32[8,8]{1,0:T(8,128)S(1)} %broadcast_subtract_fusion.lists_ref, bf16[8,4096]{1,0:T(8,128)(2,1)S(1)} %copy-done.2, bf16[64,4096]{1,0:T(8,128)(2,1)S(1)} %copy-done.1, bf16[8,512,256]{2,1,0:T(8,128)(2,1)S(1)} %copy-done, ...), custom_call_target="tpu_custom_call" | custom-call | flops 25769803776 | bytes 3145728 | tf_op jit(solution)/shard_map/pallas_call | solution.py:374
  63.6 0.0 copy-done.3
  63.6 0.0 copy-done.5
  63.6 33.5 %shard_map.78 = (f32[64,4096]{1,0:T(8,128)}, f32[64,4096]{1,0:T(8,128)}) custom-call(s32[8,12]{1,0:T(8,128)S(1)} %copy-done.5, bf16[8,4096]{1,0:T(8,128)(2,1)S(1)} %copy-done.3, f32[64,4096]{1,0:T(8,128)S(1)} %get-tuple-element.5.near_kernel_ref, f32[64,4096]{1,0:T(8,128)S(1)} %get-tuple-element.6.near_slope_ref, ...), custom_call_target="tpu_custom_call" | custom-call | flops 19327352832 | bytes 3145728 | tf_op jit(solution)/shard_map/pallas_call | solution.py:401
Async XLA Ops:
  1.3 1.6 %copy-start = (bf16[8,512,256]{2,1,0:T(8,128)(2,1)S(1)}, bf16[8,512,256]{2,1,0:T(8,128)(2,1)}, u32[]{:S(2)}) copy-start(bf16[8,512,256]{2,1,0:T(8,128)(2,1)} %interpolation_ref.1) | copy-start | bytes 6291460
  2.9 1.0 %copy-start.1 = (bf16[64,4096]{1,0:T(8,128)(2,1)S(1)}, bf16[64,4096]{1,0:T(8,128)(2,1)}, u32[]{:S(2)}) copy-start(bf16[64,4096]{1,0:T(8,128)(2,1)} %weights_ref.1) | copy-start | bytes 1572868
  4.0 0.8 copy-start.2
  4.8 0.7 copy-start.4
  5.5 58.1 %copy-start.3 = (bf16[8,4096]{1,0:T(8,128)(2,1)S(1)}, bf16[8,4096]{1,0:T(8,128)(2,1)}, u32[]{:S(2)}) copy-start(bf16[8,4096]{1,0:T(8,128)(2,1)} %points_ref.3) | copy-start | bytes 196612
  5.5 58.1 %copy-start.5 = (s32[8,12]{1,0:T(8,128)S(1)}, s32[8,12]{1,0:T(8,128)}, u32[]{:S(2)}) copy-start(s32[8,12]{1,0:T(8,128)} %lists_ref.1) | copy-start | bytes 1156

commit v3 on v2

--- a/solution.py
+++ b/solution.py
@@ -33,22 +33,23 @@
 
 def source_factor(coords):
     high, middle, low = pieces(coords * (-2.0 * rate))
-    return jnp.concatenate([high, middle, low, norm_rows(coords, 0)], axis=0).astype(jnp.bfloat16)
+    return jnp.concatenate([high, middle, low, norm_rows(coords, 0)], axis=0).T.astype(jnp.bfloat16)
 
 
 def target_factor(coords):
-    stacked = jnp.concatenate([coords, coords, coords, norm_rows(coords, 3)], axis=0)
-    return stacked.T.astype(jnp.bfloat16)
-
-
-def accumulate(targets, factor, weights):
-    exponent = jnp.dot(targets, factor, preferred_element_type=jnp.float32)
-    kernel = jnp.exp2(exponent)
-    slope = kernel * exponent
-    over_sources = (((1,), (1,)), ((), ()))
+    return jnp.concatenate([coords, coords, coords, norm_rows(coords, 3)], axis=0).astype(jnp.bfloat16)
+
+
+def products(factors, weights, targets):
+    kernels, slopes = [], []
+    for factor in factors:
+        exponent = jnp.dot(factor, targets, preferred_element_type=jnp.float32)
+        kernel = jnp.exp2(exponent)
+        kernels.append(kernel.astype(jnp.bfloat16))
+        slopes.append((kernel * exponent).astype(jnp.bfloat16))
     return (
-        lax.dot_general(kernel.astype(jnp.bfloat16), weights, over_sources, preferred_element_type=jnp.float32),
-        lax.dot_general(slope.astype(jnp.bfloat16), weights, over_sources, preferred_element_type=jnp.float32),
+        jnp.dot(weights, jnp.concatenate(kernels, axis=0), preferred_element_type=jnp.float32),
+        jnp.dot(weights, jnp.concatenate(slopes, axis=0), preferred_element_type=jnp.float32),
     )
 
 
@@ -74,13 +75,15 @@
 def near_kernel(
     count, lists_ref, points_ref, weights_ref, interpolation_ref, skeleton_ref,
     kernel_ref, slope_ref, all_ref,
-    factor_ref, weight_ref, target_ref, kernel_acc, slope_acc,
-    payload_ref, packed_ref, halo_points, halo_weights,
-    own_sem, halo_send, halo_recv, up_send, up_recv, down_send, down_recv,
+    factor_ref, weight_ref, target_ref,
+    payload_ref, packed_ref, halo_points, halo_weights, interpolation_vmem,
+    own_sem, load_sem, halo_send, halo_recv, up_send, up_recv, down_send, down_recv,
     across_send, across_recv, core_send, core_recv,
 ):
     leaves, near = lists_ref.shape
-    leaf_size = factor_ref.shape[2]
+    leaf_size = factor_ref.shape[1]
+    tile = leaf_size // 2
+    first_leaf = (lax.axis_index("leaf") - 1) * leaves
     dim = points_ref.shape[0]
     middle = packed_ref.shape[1]
     me = lax.axis_index("leaf")
@@ -98,6 +101,8 @@
             device_id={"leaf": device}, device_id_type=pl.DeviceIdType.MESH,
         )
 
+    load = pltpu.make_async_copy(interpolation_ref, interpolation_vmem, load_sem)
+    load.start()
     barrier = pltpu.get_barrier_semaphore()
 
     def greet(device):
@@ -143,7 +148,8 @@
             halo_points[side] = jnp.zeros_like(halo_points[side])
             halo_weights[side] = jnp.zeros_like(halo_weights[side])
 
-    skeleton_block(points_ref, weights_ref, interpolation_ref, skeleton_ref, payload_ref)
+    load.wait()
+    skeleton_block(points_ref, weights_ref, interpolation_vmem, skeleton_ref, payload_ref)
 
     def slot(place_of, lane_of):
         return all_ref.at[pl.ds((place_of * 4 + lane_of) * leaves, leaves)]
@@ -229,9 +235,9 @@
         factor_ref[leaves + leaf] = source_factor(coords)
         weight_ref[leaves + leaf] = weights_ref[:, columns]
         target_ref[leaf] = target_factor(coords)
-        kernel, slope = accumulate(target_ref[leaf], factor_ref[leaves + leaf], weight_ref[leaves + leaf])
-        kernel_acc[leaf] = kernel
-        slope_acc[leaf] = slope
+        kernel_ref[:, columns], slope_ref[:, columns] = products(
+            [factor_ref[leaves + leaf]], weight_ref[leaves + leaf], target_ref[leaf]
+        )
 
     for present, copies in ((has_prev, halo(0, me + 1)), (has_next, halo(1, me - 1))):
 
@@ -252,16 +258,17 @@
     def run_leaves(first, last):
         @pl.loop(first, last)
         def _(leaf):
-            @pl.loop(1, near)
-            def _(entry):
-                source = lists_ref[leaf, entry]
-                kernel, slope = accumulate(target_ref[leaf], factor_ref[source], weight_ref[source])
-                kernel_acc[leaf] += kernel
-                slope_acc[leaf] += slope
-
-            columns = pl.ds(pl.multiple_of(leaf * leaf_size, leaf_size), leaf_size)
-            kernel_ref[:, columns] = kernel_acc[leaf].T
-            slope_ref[:, columns] = slope_acc[leaf].T
+            sources = [
+                jnp.clip(lists_ref[leaf, entry] - first_leaf, 0, 3 * leaves - 1) for entry in range(1, near)
+            ]
+            weights = jnp.concatenate([weight_ref[source] for source in sources], axis=1)
+            for begin in range(0, leaf_size, tile):
+                columns = pl.ds(pl.multiple_of(leaf * leaf_size + begin, tile), tile)
+                kernel, slope = products(
+                    [factor_ref[source] for source in sources], weights, target_ref[leaf, :, begin : begin + tile]
+                )
+                kernel_ref[:, columns] += kernel
+                slope_ref[:, columns] += slope
 
     done = 0
     for step in range(1, length):
@@ -303,10 +310,11 @@
 
 def far_kernel(
     lists_ref, points_ref, near_kernel_ref, near_slope_ref, everything_ref,
-    kernel_ref, slope_ref, block_ref, kernel_acc, slope_acc, semaphore,
+    kernel_ref, slope_ref, block_ref, semaphore,
 ):
     leaves, far = lists_ref.shape
     leaf_size = points_ref.shape[1] // leaves
+    tile = leaf_size // 2
     rows = block_ref.shape[2]
     dim = points_ref.shape[0]
     rhs = kernel_ref.shape[0]
@@ -326,31 +334,23 @@
     def _(leaf):
         columns = pl.ds(pl.multiple_of(leaf * leaf_size, leaf_size), leaf_size)
         targets = target_factor(points_ref[:, columns].astype(jnp.float32))
-        kernel_acc[...] = jnp.zeros_like(kernel_acc)
-        slope_acc[...] = jnp.zeros_like(slope_acc)
-
-        @pl.loop(0, far // 2)
-        def _(pair):
-            halves = []
-            coords = []
-            for member in range(2):
-                slot = pair * 2 + member
-                fetch(leaf, slot).wait()
-                for part in range(2):
-                    halves.append(block_ref[leaf, slot, part * rhs : (part + 1) * rhs])
-                both = block_ref[leaf, slot, 2 * rhs : rows].astype(jnp.float32)
-                coords += [both[:dim], both[dim:]]
-            factor = source_factor(jnp.concatenate(coords, axis=1))
-            kernel, slope = accumulate(targets, factor, jnp.concatenate(halves, axis=1))
-            kernel_acc[...] += kernel
-            slope_acc[...] += slope
-
-        kernel_ref[:, columns] = amplitude * (near_kernel_ref[:, columns] + kernel_acc[...].T)
-        slope_ref[:, columns] = (amplitude / (length_sq * rate)) * (near_slope_ref[:, columns] + slope_acc[...].T)
+        factors, halves = [], []
+        for entry in range(far):
+            fetch(leaf, entry).wait()
+        for entry in range(far):
+            for part in range(2):
+                halves.append(block_ref[leaf, entry, part * rhs : (part + 1) * rhs])
+            both = block_ref[leaf, entry, 2 * rhs : rows].astype(jnp.float32)
+            factors.append(source_factor(jnp.concatenate([both[:dim], both[dim:]], axis=1)))
+        weights = jnp.concatenate(halves, axis=1)
+        for begin in range(0, leaf_size, tile):
+            columns = pl.ds(pl.multiple_of(leaf * leaf_size + begin, tile), tile)
+            kernel, slope = products(factors, weights, targets[:, begin : begin + tile])
+            kernel_ref[:, columns] = amplitude * (near_kernel_ref[:, columns] + kernel)
+            slope_ref[:, columns] = (amplitude / (length_sq * rate)) * (near_slope_ref[:, columns] + slope)
 
 
 def local(points, weights, interpolation, skeleton, near_lists, far_lists):
-    position = lax.axis_index("leaf")
     count = lax.axis_size("leaf")
     leaves, leaf_size, rank = interpolation.shape
     dim, rhs = points.shape[0], weights.shape[0]
@@ -367,26 +367,23 @@
         )
 
     partial = jax.ShapeDtypeStruct((rhs, width), jnp.float32)
-    accumulator = pltpu.VMEM((leaf_size, rhs), jnp.float32)
-    local_near = near_lists - (position - 1) * leaves
     dma = pltpu.SemaphoreType.DMA
     length = count // 4
     near_kernel_part, near_slope_part, everything = pl.pallas_call(
         functools.partial(near_kernel, count),
         out_shape=(partial, partial, jax.ShapeDtypeStruct((count * leaves, rows, rank // 2), jnp.bfloat16)),
-        in_specs=[smem] + [vmem] * 4,
+        in_specs=[smem, vmem, vmem, pl.BlockSpec(memory_space=pltpu.HBM), vmem],
         out_specs=(vmem, vmem, pl.BlockSpec(memory_space=pl.ANY)),
         scratch_shapes=[
-            pltpu.VMEM((3 * leaves, 4 * dim, leaf_size), jnp.bfloat16),
+            pltpu.VMEM((3 * leaves, leaf_size, 4 * dim), jnp.bfloat16),
             pltpu.VMEM((3 * leaves, rhs, leaf_size), jnp.bfloat16),
-            pltpu.VMEM((leaves, leaf_size, 4 * dim), jnp.bfloat16),
-            pltpu.VMEM((leaves, leaf_size, rhs), jnp.float32),
-            pltpu.VMEM((leaves, leaf_size, rhs), jnp.float32),
+            pltpu.VMEM((leaves, 4 * dim, leaf_size), jnp.bfloat16),
             pltpu.VMEM((leaves, rows, rank // 2), jnp.bfloat16),
             pltpu.VMEM((2 * dim, width // 2), jnp.bfloat16),
             pltpu.VMEM((2, 2 * dim, width // 2), jnp.bfloat16),
             pltpu.VMEM((2, rhs, width), jnp.bfloat16),
-            dma(()),
+            pltpu.VMEM((leaves, leaf_size, rank), jnp.bfloat16),
+            dma(()), dma(()),
             dma((2, 2)), dma((2, 2)),
             dma((length + 1,)), dma((length + 1,)), dma((length + 1,)), dma((length + 1,)),
             dma((length,)), dma((length,)),
@@ -396,7 +393,7 @@
             collective_id=0, has_side_effects=True, vmem_limit_bytes=48 * MIB
         ),
         cost_estimate=cost(near * leaf_size),
-    )(local_near, points, weights, interpolation, skeleton)
+    )(near_lists, points, weights, interpolation, skeleton)
 
     return pl.pallas_call(
         far_kernel,
@@ -405,8 +402,6 @@
         out_specs=(vmem, vmem),
         scratch_shapes=[
             pltpu.VMEM((leaves, far, rows, rank // 2), jnp.bfloat16),
-            accumulator,
-            accumulator,
             pltpu.SemaphoreType.DMA((leaves, far)),
         ],
         compiler_params=pltpu.CompilerParams(vmem_limit_bytes=48 * MIB),

time: 97.5 us -> 79.7 us (0.82)
  Pallas kernels: 91.6 us -> 73.8 us
    pallas_call x1, Pallas kernels: 33.5 us -> 23.3 us  [local(): pl.pallas_call(far_kernel, out_shape=(partial, partial), in_specs=[smem,...]
    pallas_call x1, Pallas kernels: 58.1 us -> 50.5 us  [local(): pl.pallas_call(functools.partial(near_kernel, count), out_shape=(partial,...]
    unnamed x12 -> x14, local copies, waits for them, and re-layouts: 4.17 us -> 4.85 us
where the time goes in v3:
time: 79.7 us; the launch traced here: 79.4 us
  Pallas kernels  73.8 us (93%)
  local copies, waits for them, and re-layouts  4.85 us (6%)
    pallas_call x1, Pallas kernels, local(): pl.pallas_call(functools.partial(near_kernel, count), out_shape=(partial,...  50.5 us
    pallas_call x1, Pallas kernels, local(): pl.pallas_call(far_kernel, out_shape=(partial, partial), in_specs=[smem,...  23.3 us
    unnamed x14, local copies, waits for them, and re-layouts  4.85 us

profile of v3, /device:TPU:16, one launch (start us, length us, event | category | flops | bytes accessed | tf_op | source)
XLA Modules:
  0.0 79.4 jit_solution(7020880097029695712)
XLA Ops:
  0.6 0.0 copy-start
  0.6 1.6 %copy-done = bf16[8,512,256]{2,1,0:T(8,128)(2,1)S(1)} copy-done((bf16[8,512,256]{2,1,0:T(8,128)(2,1)S(1)}, bf16[8,512,256]{2,1,0:T(8,128)(2,1)}, u32[]{:S(2)}) %copy-start) | copy-done | bytes 2097176
  2.2 0.0 copy-start.1
  2.2 1.0 %copy-done.1 = bf16[64,4096]{1,0:T(8,128)(2,1)S(1)} copy-done((bf16[64,4096]{1,0:T(8,128)(2,1)S(1)}, bf16[64,4096]{1,0:T(8,128)(2,1)}, u32[]{:S(2)}) %copy-start.1) | copy-done | bytes 524312
  3.3 0.0 copy-start.2
  3.3 0.8 %copy-done.2 = bf16[8,4096]{1,0:T(8,128)(2,1)S(1)} copy-done((bf16[8,4096]{1,0:T(8,128)(2,1)S(1)}, bf16[8,4096]{1,0:T(8,128)(2,1)}, u32[]{:S(2)}) %copy-start.2) | copy-done | bytes 65560
  4.1 0.0 copy-start.4
  4.1 0.7 copy-done.4
  4.8 0.0 copy-start.5
  4.8 0.7 copy-done.5
  5.5 0.0 copy-start.3
  5.5 0.0 copy-start.6
  5.5 50.5 %shard_map.77 = (f32[64,4096]{1,0:T(8,128)S(1)}, f32[64,4096]{1,0:T(8,128)S(1)}, bf16[128,144,128]{2,1,0:T(8,128)(2,1)}) custom-call(s32[8,8]{1,0:T(8,128)S(1)} %copy-done.5, bf16[8,4096]{1,0:T(8,128)(2,1)S(1)} %copy-done.2, bf16[64,4096]{1,0:T(8,128)(2,1)S(1)} %copy-done.1, bf16[8,512,256]{2,1,0:T(8,128)(2,1)S(1)} %copy-done, s32[8,256]{1,0:T(8,128)S(1)} %copy-done.4), custom_call_target="tpu_custom_call" | custom-call | flops 25769803776 | bytes 3145728 | tf_op jit(solution)/shard_map/pallas_call | solution.py:372
  56.0 0.0 copy-done.3
  56.0 0.0 copy-done.6
  56.0 23.3 %shard_map.78 = (f32[64,4096]{1,0:T(8,128)}, f32[64,4096]{1,0:T(8,128)}) custom-call(s32[8,12]{1,0:T(8,128)S(1)} %copy-done.6, bf16[8,4096]{1,0:T(8,128)(2,1)S(1)} %copy-done.3, f32[64,4096]{1,0:T(8,128)S(1)} %get-tuple-element.5.near_kernel_ref, f32[64,4096]{1,0:T(8,128)S(1)} %get-tuple-element.6.near_slope_ref, ...), custom_call_target="tpu_custom_call" | custom-call | flops 19327352832 | bytes 3145728 | tf_op jit(solution)/shard_map/pallas_call | solution.py:398
Async XLA Ops:
  0.6 1.6 %copy-start = (bf16[8,512,256]{2,1,0:T(8,128)(2,1)S(1)}, bf16[8,512,256]{2,1,0:T(8,128)(2,1)}, u32[]{:S(2)}) copy-start(bf16[8,512,256]{2,1,0:T(8,128)(2,1)} %interpolation_ref.1) | copy-start | bytes 6291460
  2.2 1.0 %copy-start.1 = (bf16[64,4096]{1,0:T(8,128)(2,1)S(1)}, bf16[64,4096]{1,0:T(8,128)(2,1)}, u32[]{:S(2)}) copy-start(bf16[64,4096]{1,0:T(8,128)(2,1)} %weights_ref.1) | copy-start | bytes 1572868
  3.3 0.8 %copy-start.2 = (bf16[8,4096]{1,0:T(8,128)(2,1)S(1)}, bf16[8,4096]{1,0:T(8,128)(2,1)}, u32[]{:S(2)}) copy-start(bf16[8,4096]{1,0:T(8,128)(2,1)} %points_ref.3) | copy-start | bytes 196612
  4.1 0.7 copy-start.4
  4.8 0.7 copy-start.5
  5.5 50.5 %copy-start.3 = (bf16[8,4096]{1,0:T(8,128)(2,1)S(1)}, bf16[8,4096]{1,0:T(8,128)(2,1)}, u32[]{:S(2)}) copy-start(bf16[8,4096]{1,0:T(8,128)(2,1)} %points_ref.3) | copy-start | bytes 196612
  5.5 50.5 %copy-start.6 = (s32[8,12]{1,0:T(8,128)S(1)}, s32[8,12]{1,0:T(8,128)}, u32[]{:S(2)}) copy-start(s32[8,12]{1,0:T(8,128)} %lists_ref.3) | copy-start | bytes 1156

commit v4 on v3

--- a/solution.py
+++ b/solution.py
@@ -76,7 +76,7 @@
     count, lists_ref, points_ref, weights_ref, interpolation_ref, skeleton_ref,
     kernel_ref, slope_ref, all_ref,
     factor_ref, weight_ref, target_ref,
-    payload_ref, packed_ref, halo_points, halo_weights, interpolation_vmem,
+    payload_ref, packed_ref, halo_points, halo_weights, weights_vmem, skeleton_vmem, interpolation_vmem,
     own_sem, load_sem, halo_send, halo_recv, up_send, up_recv, down_send, down_recv,
     across_send, across_recv, core_send, core_recv,
 ):
@@ -101,8 +101,14 @@
             device_id={"leaf": device}, device_id_type=pl.DeviceIdType.MESH,
         )
 
-    load = pltpu.make_async_copy(interpolation_ref, interpolation_vmem, load_sem)
-    load.start()
+    loads = [
+        pltpu.make_async_copy(source, target, load_sem.at[at])
+        for at, (source, target) in enumerate(
+            ((weights_ref, weights_vmem), (skeleton_ref, skeleton_vmem), (interpolation_ref, interpolation_vmem))
+        )
+    ]
+    for load in loads:
+        load.start()
     barrier = pltpu.get_barrier_semaphore()
 
     def greet(device):
@@ -148,8 +154,9 @@
             halo_points[side] = jnp.zeros_like(halo_points[side])
             halo_weights[side] = jnp.zeros_like(halo_weights[side])
 
-    load.wait()
-    skeleton_block(points_ref, weights_ref, interpolation_vmem, skeleton_ref, payload_ref)
+    for load in loads:
+        load.wait()
+    skeleton_block(points_ref, weights_vmem, interpolation_vmem, skeleton_vmem, payload_ref)
 
     def slot(place_of, lane_of):
         return all_ref.at[pl.ds((place_of * 4 + lane_of) * leaves, leaves)]
@@ -233,7 +240,7 @@
         columns = pl.ds(pl.multiple_of(leaf * leaf_size, leaf_size), leaf_size)
         coords = points_ref[:, columns].astype(jnp.float32)
         factor_ref[leaves + leaf] = source_factor(coords)
-        weight_ref[leaves + leaf] = weights_ref[:, columns]
+        weight_ref[leaves + leaf] = weights_vmem[:, columns]
         target_ref[leaf] = target_factor(coords)
         kernel_ref[:, columns], slope_ref[:, columns] = products(
             [factor_ref[leaves + leaf]], weight_ref[leaves + leaf], target_ref[leaf]
@@ -324,17 +331,20 @@
             everything_ref.at[lists_ref[leaf, slot]], block_ref.at[leaf, slot], semaphore.at[leaf, slot]
         )
 
-    @pl.loop(0, leaves)
-    def _(leaf):
-        @pl.loop(0, far)
-        def _(slot):
-            fetch(leaf, slot).start()
+    for entry in range(far):
+        fetch(0, entry).start()
 
     @pl.loop(0, leaves)
     def _(leaf):
         columns = pl.ds(pl.multiple_of(leaf * leaf_size, leaf_size), leaf_size)
         targets = target_factor(points_ref[:, columns].astype(jnp.float32))
         factors, halves = [], []
+
+        @pl.when(leaf + 1 < leaves)
+        def _():
+            for entry in range(far):
+                fetch(leaf + 1, entry).start()
+
         for entry in range(far):
             fetch(leaf, entry).wait()
         for entry in range(far):
@@ -372,7 +382,7 @@
     near_kernel_part, near_slope_part, everything = pl.pallas_call(
         functools.partial(near_kernel, count),
         out_shape=(partial, partial, jax.ShapeDtypeStruct((count * leaves, rows, rank // 2), jnp.bfloat16)),
-        in_specs=[smem, vmem, vmem, pl.BlockSpec(memory_space=pltpu.HBM), vmem],
+        in_specs=[smem, vmem] + [pl.BlockSpec(memory_space=pltpu.HBM)] * 3,
         out_specs=(vmem, vmem, pl.BlockSpec(memory_space=pl.ANY)),
         scratch_shapes=[
             pltpu.VMEM((3 * leaves, leaf_size, 4 * dim), jnp.bfloat16),
@@ -382,8 +392,10 @@
             pltpu.VMEM((2 * dim, width // 2), jnp.bfloat16),
             pltpu.VMEM((2, 2 * dim, width // 2), jnp.bfloat16),
             pltpu.VMEM((2, rhs, width), jnp.bfloat16),
+            pltpu.VMEM((rhs, width), jnp.bfloat16),
+            pltpu.VMEM((leaves, rank), jnp.int32),
             pltpu.VMEM((leaves, leaf_size, rank), jnp.bfloat16),
-            dma(()), dma(()),
+            dma(()), dma((3,)),
             dma((2, 2)), dma((2, 2)),
             dma((length + 1,)), dma((length + 1,)), dma((length + 1,)), dma((length + 1,)),
             dma((length,)), dma((length,)),

time: 79.7 us -> 80 us (level)
  no operation moved by 1% of the time
where the time goes in v4:
time: 80 us; the launch traced here: 79.6 us
  Pallas kernels  74 us (92%)
  local copies, waits for them, and re-layouts  4.85 us (6%)
    pallas_call x1, Pallas kernels, local(): pl.pallas_call(functools.partial(near_kernel, count), out_shape=(partial,...  50.6 us
    pallas_call x1, Pallas kernels, local(): pl.pallas_call(far_kernel, out_shape=(partial, partial), in_specs=[smem,...  23.5 us
    unnamed x14, local copies, waits for them, and re-layouts  4.85 us

profile of v4, /device:TPU:16, one launch (start us, length us, event | category | flops | bytes accessed | tf_op | source)
XLA Modules:
  0.0 79.6 jit_solution(17818399225325920707)
XLA Ops:
  0.6 0.0 copy-start
  0.6 1.6 %copy-done = bf16[8,512,256]{2,1,0:T(8,128)(2,1)S(1)} copy-done((bf16[8,512,256]{2,1,0:T(8,128)(2,1)S(1)}, bf16[8,512,256]{2,1,0:T(8,128)(2,1)}, u32[]{:S(2)}) %copy-start) | copy-done | bytes 2097176
  2.2 0.0 copy-start.1
  2.2 1.0 %copy-done.1 = bf16[64,4096]{1,0:T(8,128)(2,1)S(1)} copy-done((bf16[64,4096]{1,0:T(8,128)(2,1)S(1)}, bf16[64,4096]{1,0:T(8,128)(2,1)}, u32[]{:S(2)}) %copy-start.1) | copy-done | bytes 524312
  3.3 0.0 copy-start.2
  3.3 0.8 %copy-done.2 = bf16[8,4096]{1,0:T(8,128)(2,1)S(1)} copy-done((bf16[8,4096]{1,0:T(8,128)(2,1)S(1)}, bf16[8,4096]{1,0:T(8,128)(2,1)}, u32[]{:S(2)}) %copy-start.2) | copy-done | bytes 65560
  4.1 0.0 copy-start.4
  4.1 0.7 copy-done.4
  4.8 0.0 copy-start.5
  4.8 0.7 copy-done.5
  5.5 0.0 copy-start.3
  5.5 0.0 copy-start.6
  5.5 50.6 %shard_map.77 = (f32[64,4096]{1,0:T(8,128)S(1)}, f32[64,4096]{1,0:T(8,128)S(1)}, bf16[128,144,128]{2,1,0:T(8,128)(2,1)}) custom-call(s32[8,8]{1,0:T(8,128)S(1)} %copy-done.5, bf16[8,4096]{1,0:T(8,128)(2,1)S(1)} %copy-done.2, bf16[64,4096]{1,0:T(8,128)(2,1)S(1)} %copy-done.1, bf16[8,512,256]{2,1,0:T(8,128)(2,1)S(1)} %copy-done, s32[8,256]{1,0:T(8,128)S(1)} %copy-done.4), custom_call_target="tpu_custom_call" | custom-call | flops 25769803776 | bytes 3145728 | tf_op jit(solution)/shard_map/pallas_call | solution.py:382
  56.1 0.0 copy-done.3
  56.1 0.0 copy-done.6
  56.1 23.5 %shard_map.78 = (f32[64,4096]{1,0:T(8,128)}, f32[64,4096]{1,0:T(8,128)}) custom-call(s32[8,12]{1,0:T(8,128)S(1)} %copy-done.6, bf16[8,4096]{1,0:T(8,128)(2,1)S(1)} %copy-done.3, f32[64,4096]{1,0:T(8,128)S(1)} %get-tuple-element.5.near_kernel_ref, f32[64,4096]{1,0:T(8,128)S(1)} %get-tuple-element.6.near_slope_ref, ...), custom_call_target="tpu_custom_call" | custom-call | flops 19327352832 | bytes 3145728 | tf_op jit(solution)/shard_map/pallas_call | solution.py:410
Async XLA Ops:
  0.6 1.6 %copy-start = (bf16[8,512,256]{2,1,0:T(8,128)(2,1)S(1)}, bf16[8,512,256]{2,1,0:T(8,128)(2,1)}, u32[]{:S(2)}) copy-start(bf16[8,512,256]{2,1,0:T(8,128)(2,1)} %interpolation_ref.1) | copy-start | bytes 6291460
  2.2 1.0 %copy-start.1 = (bf16[64,4096]{1,0:T(8,128)(2,1)S(1)}, bf16[64,4096]{1,0:T(8,128)(2,1)}, u32[]{:S(2)}) copy-start(bf16[64,4096]{1,0:T(8,128)(2,1)} %weights_ref.1) | copy-start | bytes 1572868
  3.3 0.8 %copy-start.2 = (bf16[8,4096]{1,0:T(8,128)(2,1)S(1)}, bf16[8,4096]{1,0:T(8,128)(2,1)}, u32[]{:S(2)}) copy-start(bf16[8,4096]{1,0:T(8,128)(2,1)} %points_ref.3) | copy-start | bytes 196612
  4.1 0.7 copy-start.4
  4.8 0.7 copy-start.5
  5.5 50.6 %copy-start.3 = (bf16[8,4096]{1,0:T(8,128)(2,1)S(1)}, bf16[8,4096]{1,0:T(8,128)(2,1)}, u32[]{:S(2)}) copy-start(bf16[8,4096]{1,0:T(8,128)(2,1)} %points_ref.3) | copy-start | bytes 196612
  5.5 50.6 %copy-start.6 = (s32[8,12]{1,0:T(8,128)S(1)}, s32[8,12]{1,0:T(8,128)}, u32[]{:S(2)}) copy-start(s32[8,12]{1,0:T(8,128)} %lists_ref.3) | copy-start | bytes 1156
